TPU v7x, 32 devices: a whole 2x2x4 slice. The times are simulated.
32 devices in a mesh: tm: 4 (over y, x), dp: 8 (over z, core).
Axes of the slice: x: 2, y: 2, z: 4, core: 2. Of those that a mesh axis runs over, the one named last changes fastest.
Arguments:
- history: bfloat16 [8, 8192, 256], P('dp', 'tm'), may hold values from -6 to 6
- now_weight: bfloat16 [256, 1024], replicated, may hold values from -0.25 to 0.25
- past_weight: bfloat16 [256, 1024], replicated, may hold values from -0.25 to 0.25
- gate_bias: float32 [1024], replicated, may hold values from -1 to 1
- residual_weight: bfloat16 [512, 256], replicated, may hold values from -0.25 to 0.25
- skip_weight: bfloat16 [512, 256], replicated, may hold values from -0.25 to 0.25
- out_cotangent: bfloat16 [8, 8192, 256], P('dp', 'tm'), may hold values from -6 to 6
- skip_cotangent: bfloat16 [8, 8192, 256], P('dp', 'tm'), may hold values from -6 to 6
Outputs:
- residual_out: bfloat16 [8, 8192, 256], P('dp', 'tm')
- skip_out: bfloat16 [8, 8192, 256], P('dp', 'tm')
- grad_input: bfloat16 [8, 8192, 256], P('dp', 'tm')
- grad_now: float32 [256, 1024], P('dp')
- grad_past: float32 [256, 1024], P('dp')
- grad_bias: float32 [1024], P('dp')
- grad_residual: float32 [512, 256], P('dp')
- skip_grad: float32 [512, 256], P('dp')
All inputs are finite; a program needn't handle non-finite values.
Results may differ from a plain program's by a relative error of at most 0.0048.
Values may be sent and summed in bfloat16 or wider, within the bound.
A program may use at most 64 MiB of HBM per device.

v0:
```python
import jax
import jax.numpy as jnp
from jax import lax
from jax.sharding import PartitionSpec as P

DILATION_STEPS = 2048


def passed_along(value, axis, steps):
    count = lax.axis_size(axis)
    leading, last = (max(0, -steps), min(count, count - steps))
    return lax.ppermute(value, axis, [(source, source + steps) for source in range(leading, last)])


def contract_rows(left, right):
    return lax.dot_general(
        left, right, (((0,), (0,)), ((), ())), preferred_element_type=jnp.float32
    )


def shards(
    history,
    now_weight,
    past_weight,
    gate_bias,
    residual_weight,
    skip_weight,
    out_cotangent,
    skip_cotangent,
):
    histories, series_length, channels = history.shape
    gated_width = residual_weight.shape[0]
    total_rows = histories * series_length
    received_rows = passed_along(history, "tm", 1)
    lagged_input = jnp.concatenate(
        [received_rows, history[:, : series_length - DILATION_STEPS, :]], axis=1
    )
    power_series = history.reshape(total_rows, channels)
    delayed_flat = lagged_input.reshape(total_rows, channels)
    out_cot = out_cotangent.reshape(total_rows, channels)
    skip_cot = skip_cotangent.reshape(total_rows, channels)
    zeta = jnp.dot(power_series, now_weight, preferred_element_type=jnp.float32)
    zeta = zeta + jnp.dot(delayed_flat, past_weight, preferred_element_type=jnp.float32) + gate_bias
    tanh_part = jnp.tanh(zeta[:, :gated_width])
    sigm_part = jax.nn.sigmoid(zeta[:, gated_width:])
    gated = (tanh_part * sigm_part).astype(jnp.bfloat16)
    resid = (
        power_series.astype(jnp.float32)
        + jnp.dot(gated, residual_weight, preferred_element_type=jnp.float32)
    ).astype(jnp.bfloat16)
    skipped = jnp.dot(gated, skip_weight, preferred_element_type=jnp.float32).astype(jnp.bfloat16)
    dgated = jnp.dot(out_cot, residual_weight.T, preferred_element_type=jnp.float32)
    dgated = dgated + jnp.dot(skip_cot, skip_weight.T, preferred_element_type=jnp.float32)
    dzeta = jnp.concatenate(
        [
            dgated * sigm_part * (1.0 - tanh_part * tanh_part),
            dgated * tanh_part * sigm_part * (1.0 - sigm_part),
        ],
        axis=1,
    ).astype(jnp.bfloat16)
    dzeta_seq = dzeta.reshape(histories, series_length, 2 * gated_width)
    reverse_pass = jnp.einsum(
        "btk,ck->btc", dzeta_seq, past_weight, preferred_element_type=jnp.float32
    ).astype(jnp.bfloat16)
    came = passed_along(reverse_pass, "tm", -1)
    local_slice = reverse_pass[:, DILATION_STEPS:, :]
    shifted_rows = jnp.concatenate([local_slice, came], axis=1).reshape(total_rows, channels)
    shifted_rows = lax.optimization_barrier(shifted_rows).astype(jnp.float32)
    grad_in = (
        out_cot.astype(jnp.float32)
        + jnp.dot(dzeta, now_weight.T, preferred_element_type=jnp.float32)
        + shifted_rows
    )
    grad_in = grad_in.astype(jnp.bfloat16)
    partials = (
        contract_rows(power_series, dzeta),
        contract_rows(delayed_flat, dzeta),
        jnp.sum(dzeta.astype(jnp.float32), axis=0),
        contract_rows(gated, out_cot),
        contract_rows(gated, skip_cot),
    )
    summed = lax.psum((partials[0], partials[1], partials[2], partials[3], partials[4]), "tm")
    totals = (
        lax.psum_scatter(summed[0], "dp", scatter_dimension=0, tiled=True),
        lax.psum_scatter(summed[1], "dp", scatter_dimension=0, tiled=True),
        lax.psum_scatter(summed[2], "dp", scatter_dimension=0, tiled=True),
        lax.psum_scatter(summed[3], "dp", scatter_dimension=0, tiled=True),
        lax.psum_scatter(summed[4], "dp", scatter_dimension=0, tiled=True),
    )
    shape_out = (histories, series_length, channels)
    return (
        resid.reshape(shape_out),
        skipped.reshape(shape_out),
        grad_in.reshape(shape_out),
        totals[0],
        totals[1],
        totals[2],
        totals[3],
        totals[4],
    )


def solution(mesh):
    in_specs = (
        P("dp", "tm", None),
        P(),
        P(),
        P(),
        P(),
        P(),
        P("dp", "tm", None),
        P("dp", "tm", None),
    )
    out_specs = (
        P("dp", "tm", None),
        P("dp", "tm", None),
        P("dp", "tm", None),
        P("dp", None),
        P("dp", None),
        P("dp"),
        P("dp", None),
        P("dp", None),
    )
    return jax.shard_map(shards, mesh=mesh, in_specs=in_specs, out_specs=out_specs, check_vma=False)
```

profile of v0, /device:TPU:0, one launch (start us, length us, event | category | flops | bytes accessed | tf_op | source)
XLA Modules:
  0.0 246.9 jit_solution(2899875503139978124)
XLA Ops:
  7.3 5.0 %collective-permute-start = (bf16[1,2048,256]{2,1,0:T(8,128)(2,1)}, bf16[1,2048,256]{2,1,0:T(8,128)(2,1)S(1)}, u32[]{:S(2)}, u32[]{:S(2)}) collective-permute-start(bf16[1,2048,256]{2,1,0:T(8,128)(2,1)} %param.8), channel_id=1, source_target_pairs={{0,8},{8,16},{16,24},{1,9},{9,17},{17,25},{2,10},{10,18},{18,26},{... | collective-permute-start | bytes 3145736 | tf_op jit(solution)/shard_map/ppermute | solution.py:12
  12.3 2.0 fusion.13
  15.7 19.3 %collective-permute-done = bf16[1,2048,256]{2,1,0:T(8,128)(2,1)S(1)} collective-permute-done((bf16[1,2048,256]{2,1,0:T(8,128)(2,1)}, bf16[1,2048,256]{2,1,0:T(8,128)(2,1)S(1)}, u32[]{:S(2)}, u32[]{:S(2)}) %collective-permute-start) | collective-permute-done | bytes 1048608 | tf_op jit(solution)/shard_map/ppermute | solution.py:12
  36.5 4.0 %multiply_convert_fusion.1 = (bf16[2048,512]{0,1:T(8,128)(2,1)S(1)}, bf16[2048,512]{0,1:T(8,128)(2,1)S(1)}, bf16[2048,512]{0,1:T(8,128)(2,1)}) fusion(f32[2048,1024]{0,1:T(8,128)S(1)} %add_add_fusion, f32[2048,512]{0,1:T(8,128)S(1)} %fusion.13, bf16[512,256]{1,0:T(8,128)(2,1)S(1)} %copy-done.14, bf16[1,2048,256]{2,1,0:T(8,128)(2,1)S(1)} %copy-done), kind=kOutput, calls=%fused_computation.9 | convolution fusion | flops 553648128 | bytes 20185088 | tf_op jit(solution)/shard_map/dot_general | solution.py:53
  41.8 2.2 convolution_bitcast_fusion
  44.0 2.6 %copy.22 = f32[256,1024]{1,0:T(8,128)} copy(f32[256,1024]{0,1:T(8,128)} %convolution_bitcast_fusion) | data formatting | bytes 2097152
  46.7 4.1 %convolution_bitcast_fusion.1 = f32[256,1024]{0,1:T(8,128)} fusion(bf16[1,2048,256]{2,1,0:T(8,128)(2,1)} %param.8, bf16[2048,512]{0,1:T(8,128)(2,1)} %copy-done.4, bf16[2048,512]{0,1:T(8,128)(2,1)S(1)} %get-tuple-element.28), kind=kOutput, calls=%fused_computation.22 | convolution fusion | flops 1082130432 | bytes 6291456 | tf_op jit(solution)/shard_map/dot_general | solution.py:16
  50.8 2.6 %copy.20 = f32[256,1024]{1,0:T(8,128)} copy(f32[256,1024]{0,1:T(8,128)} %convolution_bitcast_fusion.1) | data formatting | bytes 2097152
  53.4 3.2 %fusion.8 = f32[512,256]{1,0:T(8,128)} fusion(bf16[2048,512]{0,1:T(8,128)(2,1)} %get-tuple-element.30, bf16[1,2048,256]{2,1,0:T(8,128)(2,1)S(1)} %copy-done), kind=kOutput, calls=%fused_computation.24 | convolution fusion | flops 536870912 | bytes 3670016 | tf_op jit(solution)/shard_map/dot_general | solution.py:16
  57.9 4.1 %fusion.4 = bf16[1,2048,256]{2,1,0:T(8,128)(2,1)} fusion(bf16[256,1024]{1,0:T(8,128)(2,1)} %param.10, bf16[2048,512]{0,1:T(8,128)(2,1)} %copy-done.4, bf16[2048,512]{0,1:T(8,128)(2,1)S(1)} %get-tuple-element.28), kind=kOutput, calls=%fused_computation.17 | convolution fusion | flops 1082654720 | bytes 5767168 | tf_op jit(solution)/shard_map/btk,ck->btc/dot_general | solution.py:62
  63.5 2.2 convert_reduce_fusion
  65.7 15.8 %all-reduce = f32[1024]{0:T(1024)S(1)} all-reduce(f32[1024]{0:T(1024)S(1)} %convert_reduce_fusion), channel_id=4, replica_groups=mesh['tm'=4,'dp'=8] {'dp'}, use_global_device_ids=true, to_apply=%region_6.0.clone | all-reduce | flops 1024 | bytes 8192
  81.6 14.1 %psum.42 = f32[128]{0:T(128)} all-reduce(f32[128]{0:T(128)S(1)} %dynamic-slice.1), channel_id=1, replica_groups=mesh['tm'=4,'dp'=8] {'tm'}, use_global_device_ids=true, to_apply=%region_5.0 | all-reduce | flops 128 | bytes 1024 | tf_op jit(solution)/shard_map/psum | solution.py:82
  95.7 3.1 %fusion.11 = f32[512,256]{1,0:T(8,128)} fusion(bf16[2048,512]{0,1:T(8,128)(2,1)} %get-tuple-element.30, bf16[1,2048,256]{2,1,0:T(8,128)(2,1)S(1)} %copy-done.1), kind=kOutput, calls=%fused_computation.27 | convolution fusion | flops 536870912 | bytes 3670016 | tf_op jit(solution)/shard_map/dot_general | solution.py:16
  99.0 3.5 %fusion.5 = bf16[1,2048,256]{2,1,0:T(8,128)(2,1)} fusion(bf16[2048,512]{0,1:T(8,128)(2,1)} %get-tuple-element.30, bf16[512,256]{1,0:T(8,128)(2,1)} %param.13), kind=kOutput, calls=%fused_computation.18 | convolution fusion | flops 537395200 | bytes 3407872 | tf_op jit(solution)/shard_map/dot_general | solution.py:51
  105.2 2.7 %convolution_add_fusion.2 = f32[2048,256]{1,0:T(8,128)} fusion(bf16[256,1024]{1,0:T(8,128)(2,1)S(1)} %copy-done.11, bf16[1,2048,256]{2,1,0:T(8,128)(2,1)S(1)} %copy-done.1, bf16[2048,512]{0,1:T(8,128)(2,1)S(1)} %copy-done.6, bf16[2048,512]{0,1:T(8,128)(2,1)S(1)} %copy-done.3), kind=kOutput, calls=%fused_computation.13 | convolution fusion | flops 1083179008 | bytes 7864320 | tf_op jit(solution)/shard_map/dot_general | solution.py:71
  108.0 1.9 copy.23
  109.9 4.4 %reduce-scatter.13.cloned.1.call-done = f32[32,1024]{1,0:T(8,128)} async-done(((f32[256,1024]{1,0:T(8,128)}), f32[32,1024]{1,0:T(8,128)}) %reduce-scatter.13.cloned.1.call-update) | async-done | bytes 131088
  114.3 1.9 copy.21
  116.2 29.7 %reduce-scatter.11.cloned.1.call-done = f32[64,256]{1,0:T(8,128)} async-done(((f32[512,256]{1,0:T(8,128)}), f32[64,256]{1,0:T(8,128)}) %reduce-scatter.11.cloned.1.call-update) | async-done | bytes 65552 | tf_op jit(solution)/shard_map/reduce_scatter | solution.py:88
  145.8 31.4 %reduce-scatter.9.cloned.1.call-done = f32[64,256]{1,0:T(8,128)} async-done(((f32[512,256]{1,0:T(8,128)}), f32[64,256]{1,0:T(8,128)}) %reduce-scatter.9.cloned.1.call-update) | async-done | bytes 65552 | tf_op jit(solution)/shard_map/reduce_scatter | solution.py:87
  177.2 3.1 %fusion.7 = bf16[1,2048,256]{2,1,0:T(8,128)(2,1)} fusion(f32[2048,256]{1,0:T(8,128)} %convolution_add_fusion.2, bf16[2048,256]{1,0:T(8,128)(2,1)} %bitcast.7), kind=kLoop, calls=%fused_computation.23 | loop fusion | flops 1572864 | bytes 4194304 | tf_op jit(solution)/shard_map/reshape | solution.py:94
  180.3 53.4 %all-reduce.4.cloned.1.call-done = (f32[32,1024]{0,1:T(8,128)}, f32[32,1024]{0,1:T(8,128)}, f32[64,256]{1,0:T(8,128)}, f32[64,256]{1,0:T(8,128)}) async-done(((f32[32,1024]{0,1:T(8,128)}, f32[32,1024]{0,1:T(8,128)}, f32[64,256]{1,0:T(8,128)}, f32[64,256]{1,0:T(8,128)}), (f32[32,1024]{0,1:T(8,128)}, f32[32,1024]{0,1:T(8,128)}, f32[64,256]{1,0:T(8,128)}, f32[64,256]{1,0:T(8,128)})) %all-reduce.4.cloned.1.call-update) | async-done | bytes 393232 | tf_op jit(solution)/shard_map/psum | solution.py:82
  233.7 1.9 copy.18
  (55 shorter events, 14.2 us)
Async XLA Ops:
  7.2 29.3 %copy-start = (bf16[1,2048,256]{2,1,0:T(8,128)(2,1)S(1)}, bf16[1,2048,256]{2,1,0:T(8,128)(2,1)}, u32[]{:S(2)}) copy-start(bf16[1,2048,256]{2,1,0:T(8,128)(2,1)} %param.15) | copy-start | bytes 3145732
  7.2 7.1 %copy-start.7 = (bf16[1,2048,256]{2,1,0:T(8,128)(2,1)S(1)}, bf16[1,2048,256]{2,1,0:T(8,128)(2,1)}, u32[]{:S(2)}) copy-start(bf16[1,2048,256]{2,1,0:T(8,128)(2,1)} %param.8) | copy-start | bytes 3145732
  7.2 7.1 %copy-start.10 = (bf16[256,1024]{1,0:T(8,128)(2,1)S(1)}, bf16[256,1024]{1,0:T(8,128)(2,1)}, u32[]{:S(2)}) copy-start(bf16[256,1024]{1,0:T(8,128)(2,1)} %param.9) | copy-start | bytes 1572868
  7.2 100.8 %reduce-scatter.15.cloned.1.call-start = ((), (), s32[]{:S(2)}) async-start(), calls=%async_computation.7 | async-start | bytes 1179648
  7.3 27.7 %collective-permute-start = (bf16[1,2048,256]{2,1,0:T(8,128)(2,1)}, bf16[1,2048,256]{2,1,0:T(8,128)(2,1)S(1)}, u32[]{:S(2)}, u32[]{:S(2)}) collective-permute-start(bf16[1,2048,256]{2,1,0:T(8,128)(2,1)} %param.8), channel_id=1, source_target_pairs={{0,8},{8,16},{16,24},{1,9},{9,17},{17,25},{2,10},{10,18},{18,26},{... | collective-permute-start | bytes 3145736 | tf_op jit(solution)/shard_map/ppermute | solution.py:12
  14.3 20.6 %copy-start.9 = (bf16[256,1024]{1,0:T(8,128)(2,1)S(1)}, bf16[256,1024]{1,0:T(8,128)(2,1)}, u32[]{:S(2)}) copy-start(bf16[256,1024]{1,0:T(8,128)(2,1)} %param.10) | copy-start | bytes 1572868
  14.3 20.6 %copy-start.13 = (f32[1024]{0:T(1024)S(1)}, f32[1024]{0:T(1024)}, u32[]{:S(2)}) copy-start(f32[1024]{0:T(1024)} %param.11) | copy-start | bytes 12292
  15.7 20.8 %copy-start.14 = (bf16[512,256]{1,0:T(8,128)(2,1)S(1)}, bf16[512,256]{1,0:T(8,128)(2,1)}, u32[]{:S(2)}) copy-start(bf16[512,256]{1,0:T(8,128)(2,1)} %param.13) | copy-start | bytes 786436
  40.4 1.3 copy-start.4
  40.4 17.5 %copy-start.2 = (bf16[2048,512]{0,1:T(8,128)(2,1)}, bf16[2048,512]{0,1:T(8,128)(2,1)S(1)}, u32[]{:S(2)}) copy-start(bf16[2048,512]{0,1:T(8,128)(2,1)S(1)} %get-tuple-element.28) | copy-start | bytes 6291460
  46.6 67.6 %reduce-scatter.13.cloned.1.call-start = ((), (), s32[]{:S(2)}) async-start(), calls=%async_computation.6 | async-start | bytes 1179648
  50.8 5.9 %copy-start.15 = (u32[32]{0:T(128)S(1)}, u32[32]{0:T(128)}, u32[]{:S(2)}) copy-start(u32[32]{0:T(128)} %constant.9) | copy-start | bytes 388
  53.4 92.5 %reduce-scatter.11.cloned.1.call-start = ((), (), s32[]{:S(2)}) async-start(), calls=%async_computation.5 | async-start | bytes 589824 | tf_op jit(solution)/shard_map/reduce_scatter | solution.py:88
  56.6 120.6 %reduce-scatter.9.cloned.1.call-start = ((), (), s32[]{:S(2)}) async-start(), calls=%async_computation.4 | async-start | bytes 589824 | tf_op jit(solution)/shard_map/reduce_scatter | solution.py:87
  57.9 5.6 %copy-start.5 = (bf16[2048,512]{0,1:T(8,128)(2,1)S(1)}, bf16[2048,512]{0,1:T(8,128)(2,1)}, u32[]{:S(2)}) copy-start(bf16[2048,512]{0,1:T(8,128)(2,1)} %copy-done.4) | copy-start | bytes 6291460
  62.1 33.6 %copy-start.1 = (bf16[1,2048,256]{2,1,0:T(8,128)(2,1)S(1)}, bf16[1,2048,256]{2,1,0:T(8,128)(2,1)}, u32[]{:S(2)}) copy-start(bf16[1,2048,256]{2,1,0:T(8,128)(2,1)} %param.14) | copy-start | bytes 3145732
  62.1 45.9 %collective-permute-start.1 = (bf16[1,2048,256]{2,1,0:T(8,128)(2,1)}, bf16[1,2048,256]{2,1,0:T(8,128)(2,1)}, u32[]{:S(2)}, u32[]{:S(2)}) collective-permute-start(bf16[1,2048,256]{2,1,0:T(8,128)(2,1)} %fusion.4), channel_id=1, source_target_pairs={{8,0},{16,8},{24,16},{9,1},{17,9},{25,17},{10,2},{18,10},{26,18},{... | collective-permute-start | bytes 3145736 | tf_op jit(solution)/shard_map/ppermute | solution.py:12
  98.8 3.8 %copy-start.8 = (bf16[1,2048,256]{2,1,0:T(8,128)(2,1)S(1)}, bf16[1,2048,256]{2,1,0:T(8,128)(2,1)}, u32[]{:S(2)}) copy-start(bf16[1,2048,256]{2,1,0:T(8,128)(2,1)} %param.8) | copy-start | bytes 3145732
  98.8 3.8 %copy-start.12 = (bf16[512,256]{1,0:T(8,128)(2,1)S(1)}, bf16[512,256]{1,0:T(8,128)(2,1)}, u32[]{:S(2)}) copy-start(bf16[512,256]{1,0:T(8,128)(2,1)} %param.12) | copy-start | bytes 786436
  98.8 134.9 %all-reduce.4.cloned.1.call-start = ((), (), s32[]{:S(2)}) async-start(), calls=%async_computation.8 | async-start | bytes 2359296 | tf_op jit(solution)/shard_map/psum | solution.py:82
  99.0 3.5 %copy-start.16 = (bf16[2048,512]{0,1:T(8,128)(2,1)S(1)}, bf16[2048,512]{0,1:T(8,128)(2,1)}, u32[]{:S(2)}) copy-start(bf16[2048,512]{0,1:T(8,128)(2,1)} %get-tuple-element.30) | copy-start | bytes 6291460
  102.6 1.8 copy-start.3
  102.6 2.6 %copy-start.6 = (bf16[2048,512]{0,1:T(8,128)(2,1)S(1)}, bf16[2048,512]{0,1:T(8,128)(2,1)}, u32[]{:S(2)}) copy-start(bf16[2048,512]{0,1:T(8,128)(2,1)} %copy-done.4) | copy-start | bytes 6291460
  102.6 2.7 %copy-start.11 = (bf16[256,1024]{1,0:T(8,128)(2,1)S(1)}, bf16[256,1024]{1,0:T(8,128)(2,1)}, u32[]{:S(2)}) copy-start(bf16[256,1024]{1,0:T(8,128)(2,1)} %param.9) | copy-start | bytes 1572868
Sparse Core Ops, SparseCore 0:
  46.8 34.5 reduce-scatter.14
  83.6 30.6 reduce-scatter.12
  116.6 29.2 reduce-scatter.10
  148.1 29.1 reduce-scatter.8
  180.4 53.2 all-reduce.3
where the time goes:
time: 248 us; the launch traced here: 247 us
  waiting for transfers between devices  138 us (56%)
  matrix products  33.5 us (14%)
  blocking collectives  29.9 us (12%)
  local copies, waits for them, and re-layouts  18.7 us (8%)
  between operations  14.6 us (6%)
  starting transfers between devices  6.84 us (3%)
  other arithmetic  5.26 us (2%)
    psum x1, waiting for transfers between devices, shards(): lax.psum((partials[0], partials[1], partials[2], partials[3], partials[4]...  53.4 us
    reduce_scatter x1, waiting for transfers between devices, shards(): lax.psum_scatter(summed[3], 'dp', scatter_dimension=0, tiled=True)  31.4 us
    reduce_scatter x1, waiting for transfers between devices, shards(): lax.psum_scatter(summed[4], 'dp', scatter_dimension=0, tiled=True)  29.7 us
    ppermute x2, waiting for transfers between devices, passed_along(): lax.ppermute(value, axis, [(source, source + steps) for source in range(l...  19.3 us
    unnamed x44, local copies, waits for them, and re-layouts  18.7 us
    unnamed x1, blocking collectives  15.8 us
    psum x1, blocking collectives, shards(): lax.psum((partials[0], partials[1], partials[2], partials[3], partials[4]...  14.1 us
    dot_general x4, matrix products, contract_rows(): lax.dot_general(left, right, (((0,), (0,)), ((), ())), preferred_element_...  12.6 us
  transfers between devices with their start and end apart: 7, of which 5 were waited for; matrix products, arithmetic and copies ran while one was open for 15% of the time, Pallas kernels for 0%

commit v1 on v0

v1 whole, which is shorter than its diff:
```python
import functools

import jax
import jax.numpy as jnp
from jax import lax
from jax.experimental import pallas as pl
from jax.experimental.pallas import tpu as pltpu
from jax.sharding import PartitionSpec as P

DILATION_STEPS = 2048
CHUNK = 512
BIAS_ROWS = 16
F32 = jnp.float32
BF16 = jnp.bfloat16
MESH = pl.DeviceIdType.MESH


def dot(a, b, dims=((1,), (0,))):
    return lax.dot_general(a, b, (dims, ((), ())), preferred_element_type=F32)


NT = ((1,), (1,))
TN = ((0,), (0,))


def layer_kernel(
    T, D,
    hist, now_w, past_w, bias, res_w, skip_w, ocot, scot,
    resid, skipped, grad_in, g_now, g_past, g_bias, g_res, g_skip,
    delayed, bw_send, bw_recv, gi_part, zn, dgs, acc_np, acc_rs, acc_b,
    a_send, a_recv, b_own, b_send, b_recv, tot, c_send, c_recv, d_buf,
    f_ss, f_rs, w_ss, w_rs, a_ss, a_rs, b_ss, b_rs, c_ss, c_rs, d_ss, d_rs,
):
    rows, C = hist.shape
    G = res_w.shape[0]
    H = D // 2
    K = rows // CHUNK
    me = lax.axis_index("tm")
    dp = lax.axis_index("dp")
    par = lax.rem(dp, 2)
    j0 = dp // 2
    up = lax.rem(me + 1, T)
    down = lax.rem(me + T - 1, T)
    has_prev = me > 0
    has_next = me < T - 1
    Rn = C // D
    Rg = G // D
    hg = Rg // 2
    W = 2 * G
    bw = W // D
    lane = W // T

    barrier = pltpu.get_barrier_semaphore()
    for o in range(1, T):
        pl.semaphore_signal(barrier, inc=1, device_id={"tm": lax.rem(me + o, T)}, device_id_type=MESH)
    for o in range(1, H):
        pl.semaphore_signal(
            barrier, inc=1, device_id={"dp": 2 * lax.rem(j0 + o, H) + par}, device_id_type=MESH
        )
    pl.semaphore_signal(barrier, inc=1, device_id={"dp": 2 * j0 + 1 - par}, device_id_type=MESH)
    pl.semaphore_wait(barrier, T - 1 + H)

    def remote(src, dst, ss, rs, target):
        return pltpu.make_async_remote_copy(
            src_ref=src, dst_ref=dst, send_sem=ss, recv_sem=rs, device_id=target, device_id_type=MESH
        )

    def fwd(c):
        s = pl.ds(pl.multiple_of(c * CHUNK, CHUNK), CHUNK)
        return remote(hist.at[s], delayed.at[s], f_ss.at[c], f_rs.at[c], {"tm": up})

    def bwd(c):
        s = pl.ds(pl.multiple_of(c * CHUNK, CHUNK), CHUNK)
        return remote(bw_send.at[s], bw_recv.at[s], w_ss.at[c], w_rs.at[c], {"tm": down})

    @pl.when(has_next)
    def _():
        for c in range(K):
            fwd(c).start()

    @pl.when(me == 0)
    def _():
        delayed[...] = jnp.zeros_like(delayed)

    @pl.when(me == T - 1)
    def _():
        bw_recv[...] = jnp.zeros_like(bw_recv)

    acc_np[...] = jnp.zeros_like(acc_np)
    acc_rs[...] = jnp.zeros_like(acc_rs)
    acc_b[...] = jnp.zeros_like(acc_b)

    def step(c, carry):
        s = pl.ds(pl.multiple_of(c * CHUNK, CHUNK), CHUNK)
        oc = ocot[s, :]
        sc = scot[s, :]
        zn[...] = dot(hist[s, :], now_w[...]) + bias[...]
        dgs[...] = dot(oc, res_w[...], NT) + dot(sc, skip_w[...], NT)

        @pl.when(has_prev)
        def _():
            fwd(c).wait_recv()

        z = zn[...] + dot(delayed[s, :], past_w[...])
        th = jnp.tanh(z[:, :G])
        sg = 0.5 * jnp.tanh(0.5 * z[:, G:]) + 0.5
        ts = th * sg
        gated = ts.astype(BF16)
        dg = dgs[...]
        dza = (dg * sg * (1.0 - th * th)).astype(BF16)
        dzb = (dg * ts * (1.0 - sg)).astype(BF16)
        dz = jnp.concatenate([dza, dzb], axis=1)
        bw_send[s, :] = dot(dz, past_w[...], NT).astype(BF16)

        @pl.when(has_prev)
        def _():
            bwd(c).start()

        acc_np[0:C, :] += dot(hist[s, :], dz, TN)
        acc_np[C:, :] += dot(delayed[s, :], dz, TN)
        acc_rs[:, 0:C] += dot(gated, oc, TN)
        acc_rs[:, C:] += dot(gated, sc, TN)
        acc_b[...] += jnp.sum(dz.astype(F32), axis=0, keepdims=True)
        resid[s, :] = (hist[s, :].astype(F32) + dot(gated, res_w[...])).astype(BF16)
        skipped[s, :] = dot(gated, skip_w[...]).astype(BF16)
        gi_part[s, :] = oc.astype(F32) + dot(dz, now_w[...], NT)
        return carry

    lax.fori_loop(0, K, step, 0)

    r1 = BIAS_ROWS
    r2 = r1 + hg
    r3 = r2 + Rn
    r4 = r3 + Rn
    for q in range(D):
        blk = b_own.at[q // 2, q % 2]
        blk[0:BIAS_ROWS, :] = jnp.zeros((BIAS_ROWS, W), F32)
        blk[0:1, 0:bw] = acc_b[:, q * bw:(q + 1) * bw]
        blk[r1:r2, 0:2 * C] = acc_rs[q * Rg:q * Rg + hg, :]
        blk[r1:r2, 2 * C:] = acc_rs[q * Rg + hg:(q + 1) * Rg, :]
        blk[r2:r3, :] = acc_np[q * Rn:(q + 1) * Rn, :]
        blk[r3:r4, :] = acc_np[C + q * Rn:C + (q + 1) * Rn, :]

    for j in range(H):
        a_send[j] = b_own[j, 1 - par].astype(BF16)
    core = remote(a_send, a_recv, a_ss, a_rs, {"dp": 2 * j0 + 1 - par})
    core.start()
    core.wait_recv()

    zs = []
    for o in range(1, H):
        jt = lax.rem(j0 + o, H)
        b_send[o - 1] = (b_own[jt, par] + a_recv[jt].astype(F32)).astype(BF16)
        cp = remote(b_send.at[o - 1], b_recv.at[o - 1], b_ss.at[o - 1], b_rs.at[o - 1], {"dp": 2 * jt + par})
        cp.start()
        zs.append(cp)
    total = b_own[j0, par] + a_recv[j0].astype(F32)
    for o in range(1, H):
        zs[o - 1].wait_recv()
        total = total + b_recv[o - 1].astype(F32)
    for t in range(T):
        tot[t] = total[:, t * lane:(t + 1) * lane]

    cs = []
    for o in range(1, T):
        t = lax.rem(me + o, T)
        c_send[o - 1] = tot[t].astype(BF16)
        cp = remote(c_send.at[o - 1], c_recv.at[o - 1], c_ss.at[o - 1], c_rs.at[o - 1], {"tm": t})
        cp.start()
        cs.append(cp)
    mine = tot[me]
    for o in range(1, T):
        cs[o - 1].wait_recv()
        mine = mine + c_recv[o - 1].astype(F32)
    d_buf[me] = mine.astype(BF16)
    ds = []
    for o in range(1, T):
        cp = remote(d_buf.at[me], d_buf.at[me], d_ss.at[o - 1], d_rs.at[o - 1], {"tm": lax.rem(me + o, T)})
        cp.start()
        ds.append(cp)

    def finish(c, carry):
        s = pl.ds(pl.multiple_of(c * CHUNK, CHUNK), CHUNK)

        @pl.when(has_next)
        def _():
            bwd(c).wait_recv()
            fwd(c).wait_send()

        grad_in[s, :] = (gi_part[s, :] + bw_recv[s, :].astype(F32)).astype(BF16)

        @pl.when(has_prev)
        def _():
            bwd(c).wait_send()

        return carry

    lax.fori_loop(0, K, finish, 0)

    for o in range(1, T):
        t = lax.rem(me + T - o, T)
        remote(d_buf.at[t], d_buf.at[t], d_ss.at[o - 1], d_rs.at[o - 1], {"tm": lax.rem(me + o, T)}).wait_recv()
    full = jnp.concatenate([d_buf[t] for t in range(T)], axis=1).astype(F32)
    g_bias[...] = full[0:1, 0:bw]
    for half in range(2):
        at = 2 * C * half
        g_res[half * hg:(half + 1) * hg, :] = full[r1:r2, at:at + C]
        g_skip[half * hg:(half + 1) * hg, :] = full[r1:r2, at + C:at + 2 * C]
    g_now[...] = full[r2:r3, :]
    g_past[...] = full[r3:r4, :]

    core.wait_send()
    for cp in zs + cs + ds:
        cp.wait_send()


def shards(T, D, history, now_weight, past_weight, gate_bias, residual_weight, skip_weight,
           out_cotangent, skip_cotangent):
    histories, steps, C = history.shape
    assert steps == DILATION_STEPS
    rows = histories * steps
    G = residual_weight.shape[0]
    W = 2 * G
    K = rows // CHUNK
    H = D // 2
    R = BIAS_ROWS + G // D // 2 + 2 * (C // D)
    lane = W // T
    flat = [x.reshape(rows, C) for x in (history, out_cotangent, skip_cotangent)]
    vmem = pl.BlockSpec(memory_space=pltpu.VMEM)
    dma = pltpu.SemaphoreType.DMA
    V = pltpu.VMEM
    outs = pl.pallas_call(
        functools.partial(layer_kernel, T, D),
        out_shape=[
            jax.ShapeDtypeStruct((rows, C), BF16),
            jax.ShapeDtypeStruct((rows, C), BF16),
            jax.ShapeDtypeStruct((rows, C), BF16),
            jax.ShapeDtypeStruct((C // D, W), F32),
            jax.ShapeDtypeStruct((C // D, W), F32),
            jax.ShapeDtypeStruct((1, W // D), F32),
            jax.ShapeDtypeStruct((G // D, C), F32),
            jax.ShapeDtypeStruct((G // D, C), F32),
        ],
        in_specs=[vmem] * 8,
        out_specs=[vmem] * 8,
        scratch_shapes=[
            V((rows, C), BF16), V((rows, C), BF16), V((rows, C), BF16), V((rows, C), F32),
            V((CHUNK, W), F32), V((CHUNK, G), F32),
            V((2 * C, W), F32), V((G, 2 * C), F32), V((1, W), F32),
            V((H, R, W), BF16), V((H, R, W), BF16), V((H, 2, R, W), F32),
            V((H - 1, R, W), BF16), V((H - 1, R, W), BF16),
            V((T, R, lane), F32), V((T - 1, R, lane), BF16), V((T - 1, R, lane), BF16),
            V((T, R, lane), BF16),
            dma((K,)), dma((K,)), dma((K,)), dma((K,)), dma, dma,
            dma((H - 1,)), dma((H - 1,)), dma((T - 1,)), dma((T - 1,)), dma((T - 1,)), dma((T - 1,)),
        ],
        compiler_params=pltpu.CompilerParams(
            collective_id=0, has_side_effects=True, vmem_limit_bytes=60 * 1024 * 1024
        ),
        cost_estimate=pl.CostEstimate(
            flops=rows * C * G * 36, bytes_accessed=rows * C * 12, transcendentals=rows * W
        ),
        name="gated_layer",
    )(flat[0], now_weight, past_weight, gate_bias.reshape(1, W), residual_weight, skip_weight, flat[1], flat[2])
    shape = (histories, steps, C)
    return (
        outs[0].reshape(shape), outs[1].reshape(shape), outs[2].reshape(shape),
        outs[3], outs[4], outs[5].reshape(W // D), outs[6], outs[7],
    )


def solution(mesh):
    seq = P("dp", "tm", None)
    return jax.shard_map(
        functools.partial(shards, mesh.shape["tm"], mesh.shape["dp"]),
        mesh=mesh,
        in_specs=(seq, P(), P(), P(), P(), P(), seq, seq),
        out_specs=(seq, seq, seq, P("dp", None), P("dp", None), P("dp"), P("dp", None), P("dp", None)),
        check_vma=False,
    )
```

time: 248 us -> 76.5 us (0.31)
  the two profiles are of different devices: /device:TPU:0 before, /device:TPU:8 now
where the time goes in v1:
time: 76.5 us; the launch traced here: 76.2 us
  Pallas kernels  66.9 us (87%)
  local copies, waits for them, and re-layouts  8.59 us (11%)
    pallas_call x1, Pallas kernels, shards(): pl.pallas_call(functools.partial(layer_kernel, T, D), out_shape=[jax.Shap...  66.9 us
    unnamed x22, local copies, waits for them, and re-layouts  8.59 us

profile of v1, /device:TPU:8, one launch (start us, length us, event | category | flops | bytes accessed | tf_op | source)
XLA Modules:
  0.0 76.2 jit_solution(4639260912219951795)
XLA Ops:
  0.6 66.9 %gated_layer.1 = (bf16[2048,256]{1,0:T(8,128)(2,1)}, bf16[2048,256]{1,0:T(8,128)(2,1)}, bf16[2048,256]{1,0:T(8,128)(2,1)}, f32[32,1024]{1,0:T(8,128)}, f32[32,10...) custom-call(bf16[2048,256]{1,0:T(8,128)(2,1)} %bitcast.11, bf16[256,1024]{1,0:T(8,128)(2,1)} %now_w.1, ...), custom_call_target="tpu_custom_call" | custom-call | flops 9663676416 | bytes 6291456 | tf_op jit(solution)/shard_map/gated_layer/pallas_call | solution.py:232
  67.6 0.0 copy-start.1
  67.6 2.4 %copy.24 = bf16[1,2048,256]{2,1,0:T(8,128)(2,1)} copy(bf16[1,2048,256]{2,1,0:T(8,128)(2,1)} %bitcast.10) | data formatting | bytes 2097152
  70.0 0.0 copy-done.1
  70.0 0.0 copy-start
  70.0 1.0 %copy.25 = bf16[1,2048,256]{2,1,0:T(8,128)(2,1)} copy(bf16[1,2048,256]{2,1,0:T(8,128)(2,1)S(1)} %bitcast.9) | data formatting | bytes 2097152
  70.9 0.6 copy-done
  71.6 0.0 copy-start.3
  71.6 1.0 %copy.26 = bf16[1,2048,256]{2,1,0:T(8,128)(2,1)} copy(bf16[1,2048,256]{2,1,0:T(8,128)(2,1)S(1)} %bitcast.8) | data formatting | bytes 2097152
  72.5 0.1 copy-done.3
  72.6 0.0 copy-start.2
  72.6 0.7 copy.27
  73.2 0.3 copy-done.2
  73.5 0.0 copy-start.6
  73.5 0.0 copy-start.5
  73.5 0.7 copy.28
  74.2 0.0 copy-done.6
  74.2 0.5 copy.29
  74.7 0.0 copy-done.5
  74.7 0.0 copy-start.4
  74.7 0.6 copy.30
  75.3 0.2 copy-done.4
  75.6 0.6 copy.31
Async XLA Ops:
  67.6 2.4 %copy-start.1 = (bf16[2048,256]{1,0:T(8,128)(2,1)S(1)}, bf16[2048,256]{1,0:T(8,128)(2,1)}, u32[]{:S(2)}) copy-start(bf16[2048,256]{1,0:T(8,128)(2,1)} %get-tuple-element.17) | copy-start | bytes 3145732
  70.0 1.6 %copy-start = (bf16[2048,256]{1,0:T(8,128)(2,1)S(1)}, bf16[2048,256]{1,0:T(8,128)(2,1)}, u32[]{:S(2)}) copy-start(bf16[2048,256]{1,0:T(8,128)(2,1)} %get-tuple-element.18) | copy-start | bytes 3145732
  71.6 1.0 %copy-start.3 = (f32[32,1024]{1,0:T(8,128)S(1)}, f32[32,1024]{1,0:T(8,128)}, u32[]{:S(2)}) copy-start(f32[32,1024]{1,0:T(8,128)} %get-tuple-element.35) | copy-start | bytes 393220
  72.6 1.0 %copy-start.2 = (f32[32,1024]{1,0:T(8,128)S(1)}, f32[32,1024]{1,0:T(8,128)}, u32[]{:S(2)}) copy-start(f32[32,1024]{1,0:T(8,128)} %get-tuple-element.36) | copy-start | bytes 393220
  73.5 0.7 copy-start.6
  73.5 1.2 %copy-start.5 = (f32[64,256]{1,0:T(8,128)S(1)}, f32[64,256]{1,0:T(8,128)}, u32[]{:S(2)}) copy-start(f32[64,256]{1,0:T(8,128)} %get-tuple-element.38) | copy-start | bytes 196612
  74.7 0.9 %copy-start.4 = (f32[64,256]{1,0:T(8,128)S(1)}, f32[64,256]{1,0:T(8,128)}, u32[]{:S(2)}) copy-start(f32[64,256]{1,0:T(8,128)} %get-tuple-element.39) | copy-start | bytes 196612

commit v2 on v1

v2 whole, which is shorter than its diff:
```python
import functools

import jax
import jax.numpy as jnp
from jax import lax
from jax.experimental import pallas as pl
from jax.experimental.pallas import tpu as pltpu
from jax.sharding import PartitionSpec as P

DILATION_STEPS = 2048
CHUNK = 512
BIAS_ROWS = 16
F32 = jnp.float32
BF16 = jnp.bfloat16
MESH = pl.DeviceIdType.MESH


def dot(a, b, dims=((1,), (0,))):
    return lax.dot_general(a, b, (dims, ((), ())), preferred_element_type=F32)


NT = ((1,), (1,))
TN = ((0,), (0,))


def layer_kernel(
    T, D,
    hist, now_w, past_w, bias, res_w, skip_w, ocot, scot,
    resid, skipped, grad_in, packed,
    delayed, bw_send, bw_recv, relay_f, relay_b, gi_part, zn, dgs, gated_s, dz_s,
    acc_np, acc_rs, acc_b, a_send, a_recv, b_own, b_send, b_recv, tot, c_send, c_recv, d_buf,
    f_ss, f_rs, w_ss, w_rs, rf_ss, rf_rs, rb_ss, rb_rs,
    a_ss, a_rs, b_ss, b_rs, c_ss, c_rs, d_ss, d_rs,
):
    rows, C = hist.shape
    G = res_w.shape[0]
    H = D // 2
    K = rows // CHUNK
    me = lax.axis_index("tm")
    dp = lax.axis_index("dp")
    par = lax.rem(dp, 2)
    j0 = dp // 2
    up = lax.rem(me + 1, T)
    down = lax.rem(me + T - 1, T)
    up2 = lax.rem(me + 2, T)
    down2 = lax.rem(me + T - 2, T)
    has_prev = me > 0
    has_next = me < T - 1
    odd = lax.rem(me, 2) == 1
    even = lax.rem(me, 2) == 0
    Rn = C // D
    Rg = G // D
    hg = Rg // 2
    W = 2 * G
    bw = W // D
    lane = W // T
    r1, r2, r3, r4 = marks(C, G, D)
    pieces = [(0, r1), (r1, r3), (r3, r4)]

    barrier = pltpu.get_barrier_semaphore()
    for o in range(1, T):
        pl.semaphore_signal(barrier, inc=1, device_id={"tm": lax.rem(me + o, T)}, device_id_type=MESH)
    for o in range(1, H):
        pl.semaphore_signal(
            barrier, inc=1, device_id={"dp": 2 * lax.rem(j0 + o, H) + par}, device_id_type=MESH
        )
    pl.semaphore_signal(barrier, inc=1, device_id={"dp": 2 * j0 + 1 - par}, device_id_type=MESH)
    pl.semaphore_wait(barrier, T - 1 + H)

    def remote(src, dst, ss, rs, target):
        return pltpu.make_async_remote_copy(
            src_ref=src, dst_ref=dst, send_sem=ss, recv_sem=rs, device_id=target, device_id_type=MESH
        )

    def span(c):
        if isinstance(c, int):
            return pl.ds(c * CHUNK, CHUNK)
        return pl.ds(pl.multiple_of(c * CHUNK, CHUNK), CHUNK)

    def fwd(c):
        return remote(hist.at[span(c)], delayed.at[span(c)], f_ss.at[c], f_rs.at[c], {"tm": up})

    def fwd_in(r):
        return remote(hist.at[span(2 * r + 1)], relay_f.at[r], f_ss.at[2 * r + 1], rf_rs.at[r], {"tm": up2})

    def fwd_out(r):
        return remote(relay_f.at[r], delayed.at[span(2 * r + 1)], rf_ss.at[r], f_rs.at[2 * r + 1], {"tm": down})

    def bwd(c):
        return remote(bw_send.at[span(c)], bw_recv.at[span(c)], w_ss.at[c], w_rs.at[c], {"tm": down})

    def bwd_in(r):
        return remote(bw_send.at[span(2 * r + 1)], relay_b.at[r], w_ss.at[2 * r + 1], rb_rs.at[r], {"tm": down2})

    def bwd_out(r):
        return remote(relay_b.at[r], bw_recv.at[span(2 * r + 1)], rb_ss.at[r], w_rs.at[2 * r + 1], {"tm": up})

    relays_f = jnp.logical_and(odd, me >= 3)
    relays_b = jnp.logical_and(even, me < T - 2)
    for c in range(K):
        if c % 2 == 0:
            @pl.when(has_next)
            def _():
                fwd(c).start()
        else:
            @pl.when(even)
            def _():
                fwd(c).start()

            @pl.when(jnp.logical_and(odd, has_next))
            def _():
                fwd_in(c // 2).start()

    @pl.when(me == 0)
    def _():
        delayed[...] = jnp.zeros_like(delayed)

    @pl.when(me == T - 1)
    def _():
        bw_recv[...] = jnp.zeros_like(bw_recv)

    acc_np[...] = jnp.zeros_like(acc_np)
    acc_rs[...] = jnp.zeros_like(acc_rs)
    acc_b[...] = jnp.zeros_like(acc_b)

    def before(c):
        s = span(c)
        zn[...] = dot(hist[s, :], now_w[...]) + bias[...]
        dgs[...] = dot(ocot[s, :], res_w[...], NT) + dot(scot[s, :], skip_w[...], NT)

    def late(c):
        s = span(c)
        gated = gated_s[...]
        resid[s, :] = (hist[s, :].astype(F32) + dot(gated, res_w[...])).astype(BF16)
        skipped[s, :] = dot(gated, skip_w[...]).astype(BF16)
        gi_part[s, :] = ocot[s, :].astype(F32) + dot(dz_s[...], now_w[...], NT)

    def core_part(c):
        s = span(c)

        @pl.when(has_prev)
        def _():
            fwd(c).wait_recv()

        z = zn[...] + dot(delayed[s, :], past_w[...])
        th = jnp.tanh(z[:, :G])
        sg = 0.5 * jnp.tanh(0.5 * z[:, G:]) + 0.5
        ts = th * sg
        gated_s[...] = ts.astype(BF16)
        dg = dgs[...]
        dz_s[:, :G] = (dg * sg * (1.0 - th * th)).astype(BF16)
        dz_s[:, G:] = (dg * ts * (1.0 - sg)).astype(BF16)
        bw_send[s, :] = dot(dz_s[...], past_w[...], NT).astype(BF16)

    def add_rs(c):
        s = span(c)
        acc_rs[:, 0:C] += dot(gated_s[...], ocot[s, :], TN)
        acc_rs[:, C:] += dot(gated_s[...], scot[s, :], TN)

    def add_now(c):
        acc_np[0:C, :] += dot(hist[span(c), :], dz_s[...], TN)
        acc_b[...] += jnp.sum(dz_s[...].astype(F32), axis=0, keepdims=True)

    def add_past(c):
        acc_np[C:, :] += dot(delayed[span(c), :], dz_s[...], TN)

    def pair(g, carry):
        for half in range(2):
            c = 2 * g + half
            before(c)
            if half == 1:
                late(c - 1)
            else:
                @pl.when(c > 0)
                def _():
                    late(c - 1)

            @pl.when(jnp.logical_and(relays_f, jnp.logical_and(c > 0, c <= K // 2)))
            def _():
                fwd_in(c - 1).wait_recv()
                fwd_out(c - 1).start()

            core_part(c)
            if half == 0:
                @pl.when(odd)
                def _():
                    bwd(c).start()
            else:
                @pl.when(odd)
                def _():
                    bwd(c).start()

                @pl.when(jnp.logical_and(even, has_prev))
                def _():
                    bwd_in(g).start()

            @pl.when(c < K - 1)
            def _():
                add_rs(c)
                add_now(c)
                add_past(c)

        return carry

    lax.fori_loop(0, K // 2, pair, 0)

    @pl.when(jnp.logical_and(even, has_prev))
    def _():
        for r in range(K // 2):
            bwd(2 * r).start()

    cores = []

    def core_send(p):
        lo, hi = pieces[p]
        for j in range(H):
            a_send[j, lo:hi, :] = b_own[j, 1 - par, lo:hi, :].astype(BF16)
        cp = remote(a_send.at[:, lo:hi, :], a_recv.at[:, lo:hi, :], a_ss.at[p], a_rs.at[p],
                    {"dp": 2 * j0 + 1 - par})
        cp.start()
        cores.append(cp)

    zs = []

    def z_send(p):
        lo, hi = pieces[p]
        cores[p].wait_recv()
        for o in range(1, H):
            jt = lax.rem(j0 + o, H)
            b_send[o - 1, lo:hi, :] = (
                b_own[jt, par, lo:hi, :] + a_recv[jt, lo:hi, :].astype(F32)
            ).astype(BF16)
            cp = remote(b_send.at[o - 1, lo:hi, :], b_recv.at[o - 1, lo:hi, :],
                        b_ss.at[p, o - 1], b_rs.at[p, o - 1], {"dp": 2 * jt + par})
            cp.start()
            zs.append(cp)

    last = K - 1
    add_rs(last)
    for q in range(D):
        b_own[q // 2, q % 2, 0:r1, 0:2 * C] = acc_rs[q * Rg:q * Rg + hg, :]
        b_own[q // 2, q % 2, 0:r1, 2 * C:] = acc_rs[q * Rg + hg:(q + 1) * Rg, :]
    core_send(0)
    add_now(last)
    for q in range(D):
        blk = b_own.at[q // 2, q % 2]
        blk[r1:r2, :] = jnp.zeros((BIAS_ROWS, W), F32)
        blk[r1:r1 + 1, 0:bw] = acc_b[:, q * bw:(q + 1) * bw]
        blk[r2:r3, :] = acc_np[q * Rn:(q + 1) * Rn, :]
    core_send(1)
    z_send(0)
    add_past(last)
    for q in range(D):
        b_own[q // 2, q % 2, r3:r4, :] = acc_np[C + q * Rn:C + (q + 1) * Rn, :]
    core_send(2)
    z_send(1)
    z_send(2)
    late(last)

    @pl.when(relays_b)
    def _():
        for r in range(K // 2):
            bwd_in(r).wait_recv()
            bwd_out(r).start()

    cs = []
    for p, (lo, hi) in enumerate(pieces):
        total = b_own[j0, par, lo:hi, :] + a_recv[j0, lo:hi, :].astype(F32)
        for o in range(1, H):
            zs[p * (H - 1) + o - 1].wait_recv()
            total = total + b_recv[o - 1, lo:hi, :].astype(F32)
        for t in range(T):
            tot[t, lo:hi, :] = total[:, t * lane:(t + 1) * lane]
        for o in range(1, T):
            t = lax.rem(me + o, T)
            c_send[o - 1, lo:hi, :] = tot[t, lo:hi, :].astype(BF16)
            cp = remote(c_send.at[o - 1, lo:hi, :], c_recv.at[o - 1, lo:hi, :],
                        c_ss.at[p, o - 1], c_rs.at[p, o - 1], {"tm": t})
            cp.start()
            cs.append(cp)

    ds = []
    for p, (lo, hi) in enumerate(pieces):
        mine = tot[me, lo:hi, :]
        for o in range(1, T):
            cs[p * (T - 1) + o - 1].wait_recv()
            mine = mine + c_recv[o - 1, lo:hi, :].astype(F32)
        d_buf[me, lo:hi, :] = mine.astype(BF16)
        for o in range(1, T):
            cp = remote(d_buf.at[me, lo:hi, :], d_buf.at[me, lo:hi, :], d_ss.at[p, o - 1], d_rs.at[p, o - 1],
                        {"tm": lax.rem(me + o, T)})
            cp.start()
            ds.append(cp)

    def finish(c, carry):
        s = span(c)

        @pl.when(has_next)
        def _():
            bwd(c).wait_recv()
            fwd(c).wait_send()

        grad_in[s, :] = (gi_part[s, :] + bw_recv[s, :].astype(F32)).astype(BF16)

        @pl.when(has_prev)
        def _():
            bwd(c).wait_send()

        return carry

    lax.fori_loop(0, K, finish, 0)

    for p, (lo, hi) in enumerate(pieces):
        for o in range(1, T):
            t = lax.rem(me + T - o, T)
            remote(d_buf.at[t, lo:hi, :], d_buf.at[t, lo:hi, :], d_ss.at[p, o - 1], d_rs.at[p, o - 1],
                   {"tm": lax.rem(me + o, T)}).wait_recv()
    for t in range(T):
        packed[:, t * lane:(t + 1) * lane] = d_buf[t]

    @pl.when(relays_f)
    def _():
        for r in range(K // 2):
            fwd_out(r).wait_send()

    @pl.when(relays_b)
    def _():
        for r in range(K // 2):
            bwd_out(r).wait_send()

    for cp in cores + zs + cs + ds:
        cp.wait_send()


def marks(C, G, D):
    r1 = G // D // 2
    r2 = r1 + BIAS_ROWS
    r3 = r2 + C // D
    return r1, r2, r3, r3 + C // D


def unpack_kernel(D, a, b, c, packed, oa, ob, oc, g_now, g_past, g_bias, g_res, g_skip, sems):
    copies = [pltpu.make_async_copy(x, y, sems.at[i]) for i, (x, y) in enumerate(((a, oa), (b, ob), (c, oc)))]
    for cp in copies:
        cp.start()
    C = a.shape[1]
    G = packed.shape[1] // 2
    r1, r2, r3, r4 = marks(C, G, D)
    g_bias[...] = packed[r1:r2, 0:2 * G // D].astype(F32)[0:1]
    for half in range(2):
        at = 2 * C * half
        g_res[half * r1:(half + 1) * r1, :] = packed[0:r1, at:at + C].astype(F32)
        g_skip[half * r1:(half + 1) * r1, :] = packed[0:r1, at + C:at + 2 * C].astype(F32)
    g_now[...] = packed[r2:r3, :].astype(F32)
    g_past[...] = packed[r3:r4, :].astype(F32)
    for cp in copies:
        cp.wait()


def shards(T, D, history, now_weight, past_weight, gate_bias, residual_weight, skip_weight,
           out_cotangent, skip_cotangent):
    histories, steps, C = history.shape
    assert steps == DILATION_STEPS
    rows = histories * steps
    G = residual_weight.shape[0]
    W = 2 * G
    K = rows // CHUNK
    H = D // 2
    R = marks(C, G, D)[3]
    lane = W // T
    flat = [x.reshape(rows, C) for x in (history, out_cotangent, skip_cotangent)]
    vmem = pl.BlockSpec(memory_space=pltpu.VMEM)
    hbm = pl.BlockSpec(memory_space=pl.ANY)
    dma = pltpu.SemaphoreType.DMA
    V = pltpu.VMEM
    seq = jax.ShapeDtypeStruct((rows, C), BF16)
    parts = pl.pallas_call(
        functools.partial(layer_kernel, T, D),
        out_shape=[seq, seq, seq, jax.ShapeDtypeStruct((R, W), BF16)],
        in_specs=[vmem] * 8,
        out_specs=[vmem] * 4,
        scratch_shapes=[
            V((rows, C), BF16), V((rows, C), BF16), V((rows, C), BF16),
            V((K // 2, CHUNK, C), BF16), V((K // 2, CHUNK, C), BF16), V((rows, C), F32),
            V((CHUNK, W), F32), V((CHUNK, G), F32), V((CHUNK, G), BF16), V((CHUNK, W), BF16),
            V((2 * C, W), F32), V((G, 2 * C), F32), V((1, W), F32),
            V((H, R, W), BF16), V((H, R, W), BF16), V((H, 2, R, W), F32),
            V((H - 1, R, W), BF16), V((H - 1, R, W), BF16),
            V((T, R, lane), F32), V((T - 1, R, lane), BF16), V((T - 1, R, lane), BF16),
            V((T, R, lane), BF16),
            dma((K,)), dma((K,)), dma((K,)), dma((K,)),
            dma((K // 2,)), dma((K // 2,)), dma((K // 2,)), dma((K // 2,)),
            dma((3,)), dma((3,)), dma((3, H - 1)), dma((3, H - 1)),
            dma((3, T - 1)), dma((3, T - 1)), dma((3, T - 1)), dma((3, T - 1)),
        ],
        compiler_params=pltpu.CompilerParams(
            collective_id=0, has_side_effects=True, vmem_limit_bytes=(28 + rows // 256) * 1024 * 1024
        ),
        cost_estimate=pl.CostEstimate(
            flops=rows * C * G * 36, bytes_accessed=rows * C * 12, transcendentals=rows * W
        ),
        name="gated_layer",
    )(flat[0], now_weight, past_weight, gate_bias.reshape(1, W), residual_weight, skip_weight, flat[1], flat[2])
    outs = pl.pallas_call(
        functools.partial(unpack_kernel, D),
        out_shape=[
            seq, seq, seq,
            jax.ShapeDtypeStruct((C // D, W), F32),
            jax.ShapeDtypeStruct((C // D, W), F32),
            jax.ShapeDtypeStruct((1, W // D), F32),
            jax.ShapeDtypeStruct((G // D, C), F32),
            jax.ShapeDtypeStruct((G // D, C), F32),
        ],
        in_specs=[hbm] * 3 + [vmem],
        out_specs=[hbm] * 3 + [vmem] * 5,
        scratch_shapes=[dma((3,))],
        compiler_params=pltpu.CompilerParams(vmem_limit_bytes=8 * 1024 * 1024),
        cost_estimate=pl.CostEstimate(flops=0, bytes_accessed=rows * C * 12, transcendentals=0),
        name="unpack_results",
    )(*parts)
    shape = (histories, steps, C)
    return (
        outs[0].reshape(shape), outs[1].reshape(shape), outs[2].reshape(shape),
        outs[3], outs[4], outs[5].reshape(W // D), outs[6], outs[7],
    )


def solution(mesh):
    seq = P("dp", "tm", None)
    return jax.shard_map(
        functools.partial(shards, mesh.shape["tm"], mesh.shape["dp"]),
        mesh=mesh,
        in_specs=(seq, P(), P(), P(), P(), P(), seq, seq),
        out_specs=(seq, seq, seq, P("dp", None), P("dp", None), P("dp"), P("dp", None), P("dp", None)),
        check_vma=False,
    )
```

time: 76.5 us -> 82.5 us (1.078)
  the two profiles are of different devices: /device:TPU:8 before, /device:TPU:0 now
where the time goes in v2:
time: 82.5 us; the launch traced here: 82.1 us
  Pallas kernels  73.1 us (89%)
  local copies, waits for them, and re-layouts  8.33 us (10%)
    pallas_call x1, Pallas kernels, shards(): pl.pallas_call(functools.partial(layer_kernel, T, D), out_shape=[seq, seq...  70.6 us
    unnamed x16, local copies, waits for them, and re-layouts  8.33 us
    pallas_call x1, Pallas kernels, shards(): pl.pallas_call(functools.partial(unpack_kernel, D), out_shape=[seq, seq,...  2.43 us

profile of v2, /device:TPU:0, one launch (start us, length us, event | category | flops | bytes accessed | tf_op | source)
XLA Modules:
  0.0 82.1 jit_solution(14748825077591258149)
XLA Ops:
  0.6 0.0 copy-start.7
  0.6 0.7 copy-done.7
  1.3 0.0 copy-start
  1.3 1.2 %copy-done = bf16[1,2048,256]{2,1,0:T(8,128)(2,1)S(1)} copy-done((bf16[1,2048,256]{2,1,0:T(8,128)(2,1)S(1)}, bf16[1,2048,256]{2,1,0:T(8,128)(2,1)}, u32[]{:S(2)}) %copy-start) | copy-done | bytes 1048600
  2.5 0.0 copy-start.1
  2.6 1.2 %copy-done.1 = bf16[1,2048,256]{2,1,0:T(8,128)(2,1)S(1)} copy-done((bf16[1,2048,256]{2,1,0:T(8,128)(2,1)S(1)}, bf16[1,2048,256]{2,1,0:T(8,128)(2,1)}, u32[]{:S(2)}) %copy-start.1) | copy-done | bytes 1048600
  3.8 0.0 copy-start.2
  3.8 1.2 %copy-done.2 = bf16[1,2048,256]{2,1,0:T(8,128)(2,1)S(1)} copy-done((bf16[1,2048,256]{2,1,0:T(8,128)(2,1)S(1)}, bf16[1,2048,256]{2,1,0:T(8,128)(2,1)}, u32[]{:S(2)}) %copy-start.2) | copy-done | bytes 1048600
  5.0 0.0 copy-start.3
  5.0 1.0 %copy-done.3 = bf16[256,1024]{1,0:T(8,128)(2,1)S(1)} copy-done((bf16[256,1024]{1,0:T(8,128)(2,1)S(1)}, bf16[256,1024]{1,0:T(8,128)(2,1)}, u32[]{:S(2)}) %copy-start.3) | copy-done | bytes 524312
  6.0 0.0 copy-start.4
  6.0 1.0 %copy-done.4 = bf16[256,1024]{1,0:T(8,128)(2,1)S(1)} copy-done((bf16[256,1024]{1,0:T(8,128)(2,1)S(1)}, bf16[256,1024]{1,0:T(8,128)(2,1)}, u32[]{:S(2)}) %copy-start.4) | copy-done | bytes 524312
  7.1 0.0 copy-start.5
  7.1 0.9 %copy-done.5 = bf16[512,256]{1,0:T(8,128)(2,1)S(1)} copy-done((bf16[512,256]{1,0:T(8,128)(2,1)S(1)}, bf16[512,256]{1,0:T(8,128)(2,1)}, u32[]{:S(2)}) %copy-start.5) | copy-done | bytes 262168
  8.0 0.0 copy-start.6
  8.0 0.9 %copy-done.6 = bf16[512,256]{1,0:T(8,128)(2,1)S(1)} copy-done((bf16[512,256]{1,0:T(8,128)(2,1)S(1)}, bf16[512,256]{1,0:T(8,128)(2,1)}, u32[]{:S(2)}) %copy-start.6) | copy-done | bytes 262168
  9.0 70.6 %gated_layer.1 = (bf16[2048,256]{1,0:T(8,128)(2,1)S(1)}, bf16[2048,256]{1,0:T(8,128)(2,1)S(1)}, bf16[2048,256]{1,0:T(8,128)(2,1)S(1)}, bf16[112,1024]{1,0:T(8,128)(2,1)S(1)}) custom-call(bf16[2048,256]{1,0:T(8,128)(2,1)S(1)} %bitcast.8, bf16[256,1024]{1,0:T(8,128)(2,1)S(1)} %copy-done.3, bf16[256,1024]{1,0:T(8,128)(2,1)S(1)} %copy-done.4, ...), custom_call_target="tpu_custom_call" | custom-call | flops 9663676416 | bytes 6291456 | tf_op jit(solution)/shard_map/gated_layer/pallas_call | solution.py:377
  79.6 2.4 %unpack_results.1 = (bf16[2048,256]{1,0:T(8,128)(2,1)}, bf16[2048,256]{1,0:T(8,128)(2,1)}, bf16[2048,256]{1,0:T(8,128)(2,1)}, f32[32,1024]{1,0:T(8,128)}, f32[32...) custom-call(bf16[2048,256]{1,0:T(8,128)(2,1)S(1)} %get-tuple-element.20.a, ...), custom_call_target="tpu_custom_call" | custom-call | bytes 6291456 | tf_op jit(solution)/shard_map/unpack_results/pallas_call | solution.py:404
Async XLA Ops:
  0.6 0.7 copy-start.7
  1.3 1.2 %copy-start = (bf16[1,2048,256]{2,1,0:T(8,128)(2,1)S(1)}, bf16[1,2048,256]{2,1,0:T(8,128)(2,1)}, u32[]{:S(2)}) copy-start(bf16[1,2048,256]{2,1,0:T(8,128)(2,1)} %param.8) | copy-start | bytes 3145732
  2.5 1.2 %copy-start.1 = (bf16[1,2048,256]{2,1,0:T(8,128)(2,1)S(1)}, bf16[1,2048,256]{2,1,0:T(8,128)(2,1)}, u32[]{:S(2)}) copy-start(bf16[1,2048,256]{2,1,0:T(8,128)(2,1)} %param.14) | copy-start | bytes 3145732
  3.8 1.2 %copy-start.2 = (bf16[1,2048,256]{2,1,0:T(8,128)(2,1)S(1)}, bf16[1,2048,256]{2,1,0:T(8,128)(2,1)}, u32[]{:S(2)}) copy-start(bf16[1,2048,256]{2,1,0:T(8,128)(2,1)} %param.15) | copy-start | bytes 3145732
  5.0 1.0 %copy-start.3 = (bf16[256,1024]{1,0:T(8,128)(2,1)S(1)}, bf16[256,1024]{1,0:T(8,128)(2,1)}, u32[]{:S(2)}) copy-start(bf16[256,1024]{1,0:T(8,128)(2,1)} %now_w.1) | copy-start | bytes 1572868
  6.0 1.0 %copy-start.4 = (bf16[256,1024]{1,0:T(8,128)(2,1)S(1)}, bf16[256,1024]{1,0:T(8,128)(2,1)}, u32[]{:S(2)}) copy-start(bf16[256,1024]{1,0:T(8,128)(2,1)} %past_w.1) | copy-start | bytes 1572868
  7.1 0.9 %copy-start.5 = (bf16[512,256]{1,0:T(8,128)(2,1)S(1)}, bf16[512,256]{1,0:T(8,128)(2,1)}, u32[]{:S(2)}) copy-start(bf16[512,256]{1,0:T(8,128)(2,1)} %res_w.1) | copy-start | bytes 786436
  8.0 0.9 %copy-start.6 = (bf16[512,256]{1,0:T(8,128)(2,1)S(1)}, bf16[512,256]{1,0:T(8,128)(2,1)}, u32[]{:S(2)}) copy-start(bf16[512,256]{1,0:T(8,128)(2,1)} %skip_w.1) | copy-start | bytes 786436

commit v3 on v2

v3 whole, which is shorter than its diff:
```python
import functools

import jax
import jax.numpy as jnp
from jax import lax
from jax.experimental import pallas as pl
from jax.experimental.pallas import tpu as pltpu
from jax.sharding import PartitionSpec as P

DILATION_STEPS = 2048
CHUNK = 512
BIAS_ROWS = 16
F32 = jnp.float32
BF16 = jnp.bfloat16
MESH = pl.DeviceIdType.MESH


def dot(a, b, dims=((1,), (0,))):
    return lax.dot_general(a, b, (dims, ((), ())), preferred_element_type=F32)


NT = ((1,), (1,))
TN = ((0,), (0,))


def layer_kernel(
    T, D,
    hist_h, now_h, past_h, bias_h, res_h, skip_h, ocot_h, scot_h,
    resid_h, skipped_h, grad_in_h, packed,
    hist, now_w, past_w, bias, res_w, skip_w, ocot, scot, resid, skipped, grad_in,
    delayed, bw_send, bw_recv, gi_part, zn, dgs, gated_s, dz_s,
    acc_np, acc_rs, acc_b, a_send, a_recv, b_own, y_send, y_recv, b_send, b_recv,
    tot, c_send, c_recv, d_buf,
    in_s, out_s, f_ss, f_rs, w_ss, w_rs,
    a_ss, a_rs, y_ss, y_rs, b_ss, b_rs, c_ss, c_rs, d_ss, d_rs,
):
    rows, C = hist.shape
    G = res_w.shape[0]
    H = D // 2
    K = rows // CHUNK
    S = T // 2
    me = lax.axis_index("tm")
    dp = lax.axis_index("dp")
    par = lax.rem(dp, 2)
    j0 = dp // 2
    up = lax.rem(me + 1, T)
    down = lax.rem(me + T - 1, T)
    has_prev = me > 0
    has_next = me < T - 1
    yb = lax.rem(me // 2, 2)
    across = me + 2 - 4 * yb
    gi = 2 * (me // 4) + lax.rem(me, 2)
    Rn = C // D
    Rg = G // D
    hg = Rg // 2
    W = 2 * G
    bw = W // D
    lane = W // T
    r1, r2, r3, r4 = marks(C, G, D)
    pieces = [(0, r1), (r1, r3), (r3, r4)]

    loads = [
        pltpu.make_async_copy(x, y, in_s.at[i])
        for i, (x, y) in enumerate((
            (hist_h, hist), (now_h, now_w), (ocot_h, ocot), (scot_h, scot),
            (res_h, res_w), (skip_h, skip_w), (past_h, past_w), (bias_h, bias),
        ))
    ]
    for cp in loads:
        cp.start()

    barrier = pltpu.get_barrier_semaphore()
    for o in range(1, T):
        pl.semaphore_signal(barrier, inc=1, device_id={"tm": lax.rem(me + o, T)}, device_id_type=MESH)
    for o in range(1, H):
        pl.semaphore_signal(
            barrier, inc=1, device_id={"dp": 2 * lax.rem(j0 + o, H) + par}, device_id_type=MESH
        )
    pl.semaphore_signal(barrier, inc=1, device_id={"dp": 2 * j0 + 1 - par}, device_id_type=MESH)

    @pl.when(me == 0)
    def _():
        delayed[...] = jnp.zeros_like(delayed)

    @pl.when(me == T - 1)
    def _():
        bw_recv[...] = jnp.zeros_like(bw_recv)

    acc_np[...] = jnp.zeros_like(acc_np)
    acc_rs[...] = jnp.zeros_like(acc_rs)
    acc_b[...] = jnp.zeros_like(acc_b)
    pl.semaphore_wait(barrier, T - 1 + H)

    def remote(src, dst, ss, rs, target):
        return pltpu.make_async_remote_copy(
            src_ref=src, dst_ref=dst, send_sem=ss, recv_sem=rs, device_id=target, device_id_type=MESH
        )

    def span(c):
        if isinstance(c, int):
            return pl.ds(c * CHUNK, CHUNK)
        return pl.ds(pl.multiple_of(c * CHUNK, CHUNK), CHUNK)

    def fwd(c):
        return remote(hist_h.at[span(c)], delayed.at[span(c)], f_ss.at[c], f_rs.at[c], {"tm": up})

    def bwd(c):
        return remote(bw_send.at[span(c)], bw_recv.at[span(c)], w_ss.at[c], w_rs.at[c], {"tm": down})

    def store(i, c):
        src, dst = ((resid, resid_h), (skipped, skipped_h), (grad_in, grad_in_h))[i]
        return pltpu.make_async_copy(src.at[span(c)], dst.at[span(c)], out_s.at[i, c])

    @pl.when(has_next)
    def _():
        for c in range(K):
            fwd(c).start()

    for cp in loads:
        cp.wait()

    def before(c):
        s = span(c)
        zn[...] = dot(hist[s, :], now_w[...]) + bias[...]
        dgs[...] = dot(ocot[s, :], res_w[...], NT) + dot(scot[s, :], skip_w[...], NT)

    def late(c):
        s = span(c)
        gated = gated_s[...]
        resid[s, :] = (hist[s, :].astype(F32) + dot(gated, res_w[...])).astype(BF16)
        skipped[s, :] = dot(gated, skip_w[...]).astype(BF16)
        gi_part[s, :] = ocot[s, :].astype(F32) + dot(dz_s[...], now_w[...], NT)
        store(0, c).start()
        store(1, c).start()

    def core_part(c):
        s = span(c)

        @pl.when(has_prev)
        def _():
            fwd(c).wait_recv()

        z = zn[...] + dot(delayed[s, :], past_w[...])
        th = jnp.tanh(z[:, :G])
        sg = 0.5 * jnp.tanh(0.5 * z[:, G:]) + 0.5
        ts = th * sg
        gated_s[...] = ts.astype(BF16)
        dg = dgs[...]
        dz_s[:, :G] = (dg * sg * (1.0 - th * th)).astype(BF16)
        dz_s[:, G:] = (dg * ts * (1.0 - sg)).astype(BF16)
        bw_send[s, :] = dot(dz_s[...], past_w[...], NT).astype(BF16)

    def add_rs(c):
        s = span(c)
        acc_rs[:, 0:C] += dot(gated_s[...], ocot[s, :], TN)
        acc_rs[:, C:] += dot(gated_s[...], scot[s, :], TN)

    def add_now(c):
        acc_np[0:C, :] += dot(hist[span(c), :], dz_s[...], TN)
        acc_b[...] += jnp.sum(dz_s[...].astype(F32), axis=0, keepdims=True)

    def add_past(c):
        acc_np[C:, :] += dot(delayed[span(c), :], dz_s[...], TN)

    def step(c, carry):
        before(c)
        core_part(c)
        add_rs(c)
        add_now(c)
        add_past(c)
        late(c)
        return carry

    last = K - 1
    lax.fori_loop(0, last, step, 0)
    before(last)
    core_part(last)

    @pl.when(has_prev)
    def _():
        for c in range(K):
            bwd(c).start()

    cores, ys, zs, cs, ds = [], [], [], [], []

    def core_send(p):
        lo, hi = pieces[p]
        for j in range(H):
            for h in range(2):
                a_send[j, h, lo:hi, :] = b_own[j, 1 - par, h, lo:hi, :].astype(BF16)
        cp = remote(a_send.at[:, :, lo:hi, :], a_recv.at[:, :, lo:hi, :], a_ss.at[p], a_rs.at[p],
                    {"dp": 2 * j0 + 1 - par})
        cp.start()
        cores.append(cp)

    def y_stage(p):
        lo, hi = pieces[p]
        cores[p].wait_recv()
        for j in range(H):
            y_send[j, lo:hi, :] = (
                b_own[j, par, 1 - yb, lo:hi, :] + a_recv[j, 1 - yb, lo:hi, :].astype(F32)
            ).astype(BF16)
        cp = remote(y_send.at[:, lo:hi, :], y_recv.at[:, lo:hi, :], y_ss.at[p], y_rs.at[p], {"tm": across})
        cp.start()
        ys.append(cp)

    def pair_sum(j, lo, hi):
        own = b_own[j, par, yb, lo:hi, :] + a_recv[j, yb, lo:hi, :].astype(F32)
        return own + y_recv[j, lo:hi, :].astype(F32)

    def z_send(p):
        lo, hi = pieces[p]
        ys[p].wait_recv()
        for o in range(1, H):
            jt = lax.rem(j0 + o, H)
            b_send[o - 1, lo:hi, :] = pair_sum(jt, lo, hi).astype(BF16)
            cp = remote(b_send.at[o - 1, lo:hi, :], b_recv.at[o - 1, lo:hi, :],
                        b_ss.at[p, o - 1], b_rs.at[p, o - 1], {"dp": 2 * jt + par})
            cp.start()
            zs.append(cp)

    def put(q, lo, hi, lanes, value):
        h = lanes // G
        at = lanes - h * G
        b_own[q // 2, q % 2, h, lo:hi, at:at + value.shape[1]] = value

    add_rs(last)
    for q in range(D):
        put(q, 0, r1, 0, acc_rs[q * Rg:q * Rg + hg, :])
        put(q, 0, r1, G, acc_rs[q * Rg + hg:(q + 1) * Rg, :])
    core_send(0)
    add_now(last)
    for q in range(D):
        for h in range(2):
            put(q, r1, r2, h * G, jnp.zeros((BIAS_ROWS, G), F32))
            put(q, r2, r3, h * G, acc_np[q * Rn:(q + 1) * Rn, h * G:(h + 1) * G])
        put(q, r1, r1 + 1, 0, acc_b[:, q * bw:(q + 1) * bw])
    core_send(1)
    y_stage(0)
    add_past(last)
    for q in range(D):
        for h in range(2):
            put(q, r3, r4, h * G, acc_np[C + q * Rn:C + (q + 1) * Rn, h * G:(h + 1) * G])
    core_send(2)
    y_stage(1)
    z_send(0)
    y_stage(2)
    z_send(1)
    late(last)
    z_send(2)

    for p, (lo, hi) in enumerate(pieces):
        total = pair_sum(j0, lo, hi)
        for o in range(1, H):
            zs[p * (H - 1) + o - 1].wait_recv()
            total = total + b_recv[o - 1, lo:hi, :].astype(F32)
        for g in range(S):
            tot[g, lo:hi, :] = total[:, g * lane:(g + 1) * lane]
        for o in range(1, S):
            g = lax.rem(gi + o, S)
            c_send[o - 1, lo:hi, :] = tot[g, lo:hi, :].astype(BF16)
            cp = remote(c_send.at[o - 1, lo:hi, :], c_recv.at[o - 1, lo:hi, :],
                        c_ss.at[p, o - 1], c_rs.at[p, o - 1],
                        {"tm": 4 * (g // 2) + 2 * yb + lax.rem(g, 2)})
            cp.start()
            cs.append(cp)

    slot = yb * S + gi
    for p, (lo, hi) in enumerate(pieces):
        mine = tot[gi, lo:hi, :]
        for o in range(1, S):
            cs[p * (S - 1) + o - 1].wait_recv()
            mine = mine + c_recv[o - 1, lo:hi, :].astype(F32)
        d_buf[slot, lo:hi, :] = mine.astype(BF16)
        for o in range(1, T):
            cp = remote(d_buf.at[slot, lo:hi, :], d_buf.at[slot, lo:hi, :], d_ss.at[p, o - 1], d_rs.at[p, o - 1],
                        {"tm": lax.rem(me + o, T)})
            cp.start()
            ds.append(cp)

    def finish(c, carry):
        s = span(c)

        @pl.when(has_next)
        def _():
            bwd(c).wait_recv()
            fwd(c).wait_send()

        grad_in[s, :] = (gi_part[s, :] + bw_recv[s, :].astype(F32)).astype(BF16)
        store(2, c).start()
        store(0, c).wait()
        store(1, c).wait()

        @pl.when(has_prev)
        def _():
            bwd(c).wait_send()

        return carry

    lax.fori_loop(0, K, finish, 0)

    for p, (lo, hi) in enumerate(pieces):
        for o in range(1, T):
            t = lax.rem(me + T - o, T)
            at = lax.rem(t // 2, 2) * S + 2 * (t // 4) + lax.rem(t, 2)
            remote(d_buf.at[at, lo:hi, :], d_buf.at[at, lo:hi, :], d_ss.at[p, o - 1], d_rs.at[p, o - 1],
                   {"tm": lax.rem(me + o, T)}).wait_recv()
    for t in range(T):
        packed[:, t * lane:(t + 1) * lane] = d_buf[t]
    for cp in cores + ys + zs + cs + ds:
        cp.wait_send()
    for c in range(K):
        store(2, c).wait()


def marks(C, G, D):
    r1 = G // D // 2
    r2 = r1 + BIAS_ROWS
    r3 = r2 + C // D
    return r1, r2, r3, r3 + C // D


def unpack_kernel(D, a, b, c, packed, oa, ob, oc, g_now, g_past, g_bias, g_res, g_skip, sems):
    copies = [pltpu.make_async_copy(x, y, sems.at[i]) for i, (x, y) in enumerate(((a, oa), (b, ob), (c, oc)))]
    for cp in copies:
        cp.start()
    C = a.shape[1]
    G = packed.shape[1] // 2
    r1, r2, r3, r4 = marks(C, G, D)
    g_bias[...] = packed[r1:r2, 0:2 * G // D].astype(F32)[0:1]
    for half in range(2):
        at = 2 * C * half
        g_res[half * r1:(half + 1) * r1, :] = packed[0:r1, at:at + C].astype(F32)
        g_skip[half * r1:(half + 1) * r1, :] = packed[0:r1, at + C:at + 2 * C].astype(F32)
    g_now[...] = packed[r2:r3, :].astype(F32)
    g_past[...] = packed[r3:r4, :].astype(F32)
    for cp in copies:
        cp.wait()


def shards(T, D, history, now_weight, past_weight, gate_bias, residual_weight, skip_weight,
           out_cotangent, skip_cotangent):
    histories, steps, C = history.shape
    assert steps == DILATION_STEPS
    rows = histories * steps
    G = residual_weight.shape[0]
    W = 2 * G
    K = rows // CHUNK
    H = D // 2
    R = marks(C, G, D)[3]
    lane = W // T
    S = T // 2
    flat = [x.reshape(rows, C) for x in (history, out_cotangent, skip_cotangent)]
    vmem = pl.BlockSpec(memory_space=pltpu.VMEM)
    hbm = pl.BlockSpec(memory_space=pl.ANY)
    dma = pltpu.SemaphoreType.DMA
    V = pltpu.VMEM
    seq = jax.ShapeDtypeStruct((rows, C), BF16)
    parts = pl.pallas_call(
        functools.partial(layer_kernel, T, D),
        out_shape=[seq, seq, seq, jax.ShapeDtypeStruct((R, W), BF16)],
        in_specs=[hbm] * 8,
        out_specs=[hbm] * 3 + [vmem],
        scratch_shapes=[
            V((rows, C), BF16), V((C, W), BF16), V((C, W), BF16), V((1, W), F32),
            V((G, C), BF16), V((G, C), BF16), V((rows, C), BF16), V((rows, C), BF16),
            V((rows, C), BF16), V((rows, C), BF16), V((rows, C), BF16),
            V((rows, C), BF16), V((rows, C), BF16), V((rows, C), BF16), V((rows, C), F32),
            V((CHUNK, W), F32), V((CHUNK, G), F32), V((CHUNK, G), BF16), V((CHUNK, W), BF16),
            V((2 * C, W), F32), V((G, 2 * C), F32), V((1, W), F32),
            V((H, 2, R, G), BF16), V((H, 2, R, G), BF16), V((H, 2, 2, R, G), F32),
            V((H, R, G), BF16), V((H, R, G), BF16),
            V((H - 1, R, G), BF16), V((H - 1, R, G), BF16),
            V((S, R, lane), F32), V((S - 1, R, lane), BF16), V((S - 1, R, lane), BF16),
            V((T, R, lane), BF16),
            dma((8,)), dma((3, K)), dma((K,)), dma((K,)), dma((K,)), dma((K,)),
            dma((3,)), dma((3,)), dma((3,)), dma((3,)), dma((3, H - 1)), dma((3, H - 1)),
            dma((3, S - 1)), dma((3, S - 1)), dma((3, T - 1)), dma((3, T - 1)),
        ],
        compiler_params=pltpu.CompilerParams(
            collective_id=0, has_side_effects=True, vmem_limit_bytes=60 * 1024 * 1024
        ),
        cost_estimate=pl.CostEstimate(
            flops=rows * C * G * 36, bytes_accessed=rows * C * 12, transcendentals=rows * W
        ),
        name="gated_layer",
    )(flat[0], now_weight, past_weight, gate_bias.reshape(1, W), residual_weight, skip_weight, flat[1], flat[2])
    outs = pl.pallas_call(
        functools.partial(unpack_kernel, D),
        out_shape=[
            seq, seq, seq,
            jax.ShapeDtypeStruct((C // D, W), F32),
            jax.ShapeDtypeStruct((C // D, W), F32),
            jax.ShapeDtypeStruct((1, W // D), F32),
            jax.ShapeDtypeStruct((G // D, C), F32),
            jax.ShapeDtypeStruct((G // D, C), F32),
        ],
        in_specs=[hbm] * 3 + [vmem],
        out_specs=[hbm] * 3 + [vmem] * 5,
        scratch_shapes=[dma((3,))],
        compiler_params=pltpu.CompilerParams(vmem_limit_bytes=60 * 1024 * 1024),
        cost_estimate=pl.CostEstimate(flops=0, bytes_accessed=rows * C * 12, transcendentals=0),
        name="unpack_results",
    )(*parts)
    shape = (histories, steps, C)
    return (
        outs[0].reshape(shape), outs[1].reshape(shape), outs[2].reshape(shape),
        outs[3], outs[4], outs[5].reshape(W // D), outs[6], outs[7],
    )


def solution(mesh):
    seq = P("dp", "tm", None)
    return jax.shard_map(
        functools.partial(shards, mesh.shape["tm"], mesh.shape["dp"]),
        mesh=mesh,
        in_specs=(seq, P(), P(), P(), P(), P(), seq, seq),
        out_specs=(seq, seq, seq, P("dp", None), P("dp", None), P("dp"), P("dp", None), P("dp", None)),
        check_vma=False,
    )
```

time: 82.5 us -> 175 us (2.12)
  Pallas kernels: 73.1 us -> 175 us
  local copies, waits for them, and re-layouts: 8.33 us -> 0 us
    pallas_call x1, Pallas kernels: 2.43 us -> 98.1 us  [shards(): pl.pallas_call(functools.partial(unpack_kernel, D), out_shape=[seq, seq,...]
    unnamed x16 -> x0, local copies, waits for them, and re-layouts: 8.33 us -> none
    pallas_call x1, Pallas kernels: 70.6 us -> 76.4 us  [shards(): pl.pallas_call(functools.partial(layer_kernel, T, D), out_shape=[seq, seq...]
where the time goes in v3:
time: 175 us
  Pallas kernels  175 us (100%)
    pallas_call x1, Pallas kernels, shards(): pl.pallas_call(functools.partial(unpack_kernel, D), out_shape=[seq, seq,...  98.1 us
    pallas_call x1, Pallas kernels, shards(): pl.pallas_call(functools.partial(layer_kernel, T, D), out_shape=[seq, seq...  76.4 us

profile of v3, /device:TPU:0, one launch (start us, length us, event | category | flops | bytes accessed | tf_op | source)
XLA Modules:
  0.0 175.2 jit_solution(14099695740848647043)
XLA Ops:
  0.6 76.4 %gated_layer.1 = (bf16[2048,256]{1,0:T(8,128)(2,1)}, bf16[2048,256]{1,0:T(8,128)(2,1)}, bf16[2048,256]{1,0:T(8,128)(2,1)}, bf16[112,1024]{1,0:T(8,128)(2,1)}) custom-call(bf16[2048,256]{1,0:T(8,128)(2,1)} %bitcast.8, bf16[256,1024]{1,0:T(8,128)(2,1)} %now_h.1, bf16[256,1024]{1,0:T(8,128)(2,1)} %past_h.1, f32[1,1024]{1,0:T(1,128)} %bitcast.14, ...), custom_call_target="tpu_custom_call" | custom-call | flops 9663676416 | bytes 6291456 | tf_op jit(solution)/shard_map/gated_layer/pallas_call | solution.py:359
  77.1 98.1 %unpack_results.1 = (bf16[2048,256]{1,0:T(8,128)(2,1)}, bf16[2048,256]{1,0:T(8,128)(2,1)}, bf16[2048,256]{1,0:T(8,128)(2,1)}, f32[32,1024]{1,0:T(8,128)}, f32[32...) custom-call(bf16[2048,256]{1,0:T(8,128)(2,1)} %get-tuple-element.20.a, ...), custom_call_target="tpu_custom_call" | custom-call | bytes 6291456 | tf_op jit(solution)/shard_map/unpack_results/pallas_call | solution.py:388

commit v4 on v3

--- a/solution.py
+++ b/solution.py
@@ -29,16 +29,15 @@
     resid_h, skipped_h, grad_in_h, packed,
     hist, now_w, past_w, bias, res_w, skip_w, ocot, scot, resid, skipped, grad_in,
     delayed, bw_send, bw_recv, gi_part, zn, dgs, gated_s, dz_s,
-    acc_np, acc_rs, acc_b, a_send, a_recv, b_own, y_send, y_recv, b_send, b_recv,
+    acc_np, acc_rs, acc_b, a_send, a_recv, b_own, b_send, b_recv,
     tot, c_send, c_recv, d_buf,
     in_s, out_s, f_ss, f_rs, w_ss, w_rs,
-    a_ss, a_rs, y_ss, y_rs, b_ss, b_rs, c_ss, c_rs, d_ss, d_rs,
+    a_ss, a_rs, b_ss, b_rs, c_ss, c_rs, d_ss, d_rs,
 ):
     rows, C = hist.shape
     G = res_w.shape[0]
     H = D // 2
     K = rows // CHUNK
-    S = T // 2
     me = lax.axis_index("tm")
     dp = lax.axis_index("dp")
     par = lax.rem(dp, 2)
@@ -47,9 +46,6 @@
     down = lax.rem(me + T - 1, T)
     has_prev = me > 0
     has_next = me < T - 1
-    yb = lax.rem(me // 2, 2)
-    across = me + 2 - 4 * yb
-    gi = 2 * (me // 4) + lax.rem(me, 2)
     Rn = C // D
     Rg = G // D
     hg = Rg // 2
@@ -89,6 +85,7 @@
     acc_np[...] = jnp.zeros_like(acc_np)
     acc_rs[...] = jnp.zeros_like(acc_rs)
     acc_b[...] = jnp.zeros_like(acc_b)
+    loads[0].wait()
     pl.semaphore_wait(barrier, T - 1 + H)
 
     def remote(src, dst, ss, rs, target):
@@ -102,7 +99,7 @@
         return pl.ds(pl.multiple_of(c * CHUNK, CHUNK), CHUNK)
 
     def fwd(c):
-        return remote(hist_h.at[span(c)], delayed.at[span(c)], f_ss.at[c], f_rs.at[c], {"tm": up})
+        return remote(hist.at[span(c)], delayed.at[span(c)], f_ss.at[c], f_rs.at[c], {"tm": up})
 
     def bwd(c):
         return remote(bw_send.at[span(c)], bw_recv.at[span(c)], w_ss.at[c], w_rs.at[c], {"tm": down})
@@ -116,25 +113,29 @@
         for c in range(K):
             fwd(c).start()
 
-    for cp in loads:
+    for cp in loads[1:]:
         cp.wait()
 
-    def before(c):
-        s = span(c)
-        zn[...] = dot(hist[s, :], now_w[...]) + bias[...]
-        dgs[...] = dot(ocot[s, :], res_w[...], NT) + dot(scot[s, :], skip_w[...], NT)
-
-    def late(c):
-        s = span(c)
-        gated = gated_s[...]
+    def before(c, carry):
+        s = span(c)
+        dgs[s, :] = dot(ocot[s, :], res_w[...], NT) + dot(scot[s, :], skip_w[...], NT)
+        return carry
+
+    lax.fori_loop(0, K, before, 0)
+
+    def late(c, carry):
+        s = span(c)
+        gated = gated_s[s, :]
         resid[s, :] = (hist[s, :].astype(F32) + dot(gated, res_w[...])).astype(BF16)
         skipped[s, :] = dot(gated, skip_w[...]).astype(BF16)
-        gi_part[s, :] = ocot[s, :].astype(F32) + dot(dz_s[...], now_w[...], NT)
+        gi_part[s, :] = ocot[s, :].astype(F32) + dot(dz_s[s, :], now_w[...], NT)
         store(0, c).start()
         store(1, c).start()
+        return carry
 
     def core_part(c):
         s = span(c)
+        zn[...] = dot(hist[s, :], now_w[...]) + bias[...]
 
         @pl.when(has_prev)
         def _():
@@ -144,73 +145,60 @@
         th = jnp.tanh(z[:, :G])
         sg = 0.5 * jnp.tanh(0.5 * z[:, G:]) + 0.5
         ts = th * sg
-        gated_s[...] = ts.astype(BF16)
-        dg = dgs[...]
-        dz_s[:, :G] = (dg * sg * (1.0 - th * th)).astype(BF16)
-        dz_s[:, G:] = (dg * ts * (1.0 - sg)).astype(BF16)
-        bw_send[s, :] = dot(dz_s[...], past_w[...], NT).astype(BF16)
+        gated_s[s, :] = ts.astype(BF16)
+        dg = dgs[s, :]
+        dza = (dg * sg * (1.0 - th * th)).astype(BF16)
+        dzb = (dg * ts * (1.0 - sg)).astype(BF16)
+        dz = jnp.concatenate([dza, dzb], axis=1)
+        dz_s[s, :] = dz
+        bw_send[s, :] = dot(dz, past_w[...], NT).astype(BF16)
+
+        @pl.when(has_prev)
+        def _():
+            bwd(c).start()
 
     def add_rs(c):
         s = span(c)
-        acc_rs[:, 0:C] += dot(gated_s[...], ocot[s, :], TN)
-        acc_rs[:, C:] += dot(gated_s[...], scot[s, :], TN)
+        acc_rs[:, 0:C] += dot(gated_s[s, :], ocot[s, :], TN)
+        acc_rs[:, C:] += dot(gated_s[s, :], scot[s, :], TN)
 
     def add_now(c):
-        acc_np[0:C, :] += dot(hist[span(c), :], dz_s[...], TN)
-        acc_b[...] += jnp.sum(dz_s[...].astype(F32), axis=0, keepdims=True)
+        s = span(c)
+        acc_np[0:C, :] += dot(hist[s, :], dz_s[s, :], TN)
+        acc_b[...] += jnp.sum(dz_s[s, :].astype(F32), axis=0, keepdims=True)
 
     def add_past(c):
-        acc_np[C:, :] += dot(delayed[span(c), :], dz_s[...], TN)
+        s = span(c)
+        acc_np[C:, :] += dot(delayed[s, :], dz_s[s, :], TN)
 
     def step(c, carry):
-        before(c)
         core_part(c)
         add_rs(c)
         add_now(c)
         add_past(c)
-        late(c)
         return carry
 
     last = K - 1
     lax.fori_loop(0, last, step, 0)
-    before(last)
     core_part(last)
 
-    @pl.when(has_prev)
-    def _():
-        for c in range(K):
-            bwd(c).start()
-
-    cores, ys, zs, cs, ds = [], [], [], [], []
+    cores, zs, cs, ds = [], [], [], []
 
     def core_send(p):
         lo, hi = pieces[p]
         for j in range(H):
-            for h in range(2):
-                a_send[j, h, lo:hi, :] = b_own[j, 1 - par, h, lo:hi, :].astype(BF16)
-        cp = remote(a_send.at[:, :, lo:hi, :], a_recv.at[:, :, lo:hi, :], a_ss.at[p], a_rs.at[p],
+            a_send[j, lo:hi, :] = b_own[j, 1 - par, lo:hi, :].astype(BF16)
+        cp = remote(a_send.at[:, lo:hi, :], a_recv.at[:, lo:hi, :], a_ss.at[p], a_rs.at[p],
                     {"dp": 2 * j0 + 1 - par})
         cp.start()
         cores.append(cp)
 
-    def y_stage(p):
+    def pair_sum(j, lo, hi):
+        return b_own[j, par, lo:hi, :] + a_recv[j, lo:hi, :].astype(F32)
+
+    def z_send(p):
         lo, hi = pieces[p]
         cores[p].wait_recv()
-        for j in range(H):
-            y_send[j, lo:hi, :] = (
-                b_own[j, par, 1 - yb, lo:hi, :] + a_recv[j, 1 - yb, lo:hi, :].astype(F32)
-            ).astype(BF16)
-        cp = remote(y_send.at[:, lo:hi, :], y_recv.at[:, lo:hi, :], y_ss.at[p], y_rs.at[p], {"tm": across})
-        cp.start()
-        ys.append(cp)
-
-    def pair_sum(j, lo, hi):
-        own = b_own[j, par, yb, lo:hi, :] + a_recv[j, yb, lo:hi, :].astype(F32)
-        return own + y_recv[j, lo:hi, :].astype(F32)
-
-    def z_send(p):
-        lo, hi = pieces[p]
-        ys[p].wait_recv()
         for o in range(1, H):
             jt = lax.rem(j0 + o, H)
             b_send[o - 1, lo:hi, :] = pair_sum(jt, lo, hi).astype(BF16)
@@ -219,61 +207,50 @@
             cp.start()
             zs.append(cp)
 
-    def put(q, lo, hi, lanes, value):
-        h = lanes // G
-        at = lanes - h * G
-        b_own[q // 2, q % 2, h, lo:hi, at:at + value.shape[1]] = value
-
     add_rs(last)
     for q in range(D):
-        put(q, 0, r1, 0, acc_rs[q * Rg:q * Rg + hg, :])
-        put(q, 0, r1, G, acc_rs[q * Rg + hg:(q + 1) * Rg, :])
+        b_own[q // 2, q % 2, 0:r1, 0:2 * C] = acc_rs[q * Rg:q * Rg + hg, :]
+        b_own[q // 2, q % 2, 0:r1, 2 * C:] = acc_rs[q * Rg + hg:(q + 1) * Rg, :]
     core_send(0)
     add_now(last)
     for q in range(D):
-        for h in range(2):
-            put(q, r1, r2, h * G, jnp.zeros((BIAS_ROWS, G), F32))
-            put(q, r2, r3, h * G, acc_np[q * Rn:(q + 1) * Rn, h * G:(h + 1) * G])
-        put(q, r1, r1 + 1, 0, acc_b[:, q * bw:(q + 1) * bw])
+        blk = b_own.at[q // 2, q % 2]
+        blk[r1:r2, :] = jnp.zeros((BIAS_ROWS, W), F32)
+        blk[r1:r1 + 1, 0:bw] = acc_b[:, q * bw:(q + 1) * bw]
+        blk[r2:r3, :] = acc_np[q * Rn:(q + 1) * Rn, :]
     core_send(1)
-    y_stage(0)
+    z_send(0)
     add_past(last)
     for q in range(D):
-        for h in range(2):
-            put(q, r3, r4, h * G, acc_np[C + q * Rn:C + (q + 1) * Rn, h * G:(h + 1) * G])
+        b_own[q // 2, q % 2, r3:r4, :] = acc_np[C + q * Rn:C + (q + 1) * Rn, :]
     core_send(2)
-    y_stage(1)
-    z_send(0)
-    y_stage(2)
     z_send(1)
-    late(last)
     z_send(2)
+    lax.fori_loop(0, K, late, 0)
 
     for p, (lo, hi) in enumerate(pieces):
         total = pair_sum(j0, lo, hi)
         for o in range(1, H):
             zs[p * (H - 1) + o - 1].wait_recv()
             total = total + b_recv[o - 1, lo:hi, :].astype(F32)
-        for g in range(S):
-            tot[g, lo:hi, :] = total[:, g * lane:(g + 1) * lane]
-        for o in range(1, S):
-            g = lax.rem(gi + o, S)
-            c_send[o - 1, lo:hi, :] = tot[g, lo:hi, :].astype(BF16)
+        for t in range(T):
+            tot[t, lo:hi, :] = total[:, t * lane:(t + 1) * lane]
+        for o in range(1, T):
+            t = lax.rem(me + o, T)
+            c_send[o - 1, lo:hi, :] = tot[t, lo:hi, :].astype(BF16)
             cp = remote(c_send.at[o - 1, lo:hi, :], c_recv.at[o - 1, lo:hi, :],
-                        c_ss.at[p, o - 1], c_rs.at[p, o - 1],
-                        {"tm": 4 * (g // 2) + 2 * yb + lax.rem(g, 2)})
+                        c_ss.at[p, o - 1], c_rs.at[p, o - 1], {"tm": t})
             cp.start()
             cs.append(cp)
 
-    slot = yb * S + gi
     for p, (lo, hi) in enumerate(pieces):
-        mine = tot[gi, lo:hi, :]
-        for o in range(1, S):
-            cs[p * (S - 1) + o - 1].wait_recv()
+        mine = tot[me, lo:hi, :]
+        for o in range(1, T):
+            cs[p * (T - 1) + o - 1].wait_recv()
             mine = mine + c_recv[o - 1, lo:hi, :].astype(F32)
-        d_buf[slot, lo:hi, :] = mine.astype(BF16)
+        d_buf[me, lo:hi, :] = mine.astype(BF16)
         for o in range(1, T):
-            cp = remote(d_buf.at[slot, lo:hi, :], d_buf.at[slot, lo:hi, :], d_ss.at[p, o - 1], d_rs.at[p, o - 1],
+            cp = remote(d_buf.at[me, lo:hi, :], d_buf.at[me, lo:hi, :], d_ss.at[p, o - 1], d_rs.at[p, o - 1],
                         {"tm": lax.rem(me + o, T)})
             cp.start()
             ds.append(cp)
@@ -302,12 +279,11 @@
     for p, (lo, hi) in enumerate(pieces):
         for o in range(1, T):
             t = lax.rem(me + T - o, T)
-            at = lax.rem(t // 2, 2) * S + 2 * (t // 4) + lax.rem(t, 2)
-            remote(d_buf.at[at, lo:hi, :], d_buf.at[at, lo:hi, :], d_ss.at[p, o - 1], d_rs.at[p, o - 1],
+            remote(d_buf.at[t, lo:hi, :], d_buf.at[t, lo:hi, :], d_ss.at[p, o - 1], d_rs.at[p, o - 1],
                    {"tm": lax.rem(me + o, T)}).wait_recv()
     for t in range(T):
         packed[:, t * lane:(t + 1) * lane] = d_buf[t]
-    for cp in cores + ys + zs + cs + ds:
+    for cp in cores + zs + cs + ds:
         cp.wait_send()
     for c in range(K):
         store(2, c).wait()
@@ -349,7 +325,6 @@
     H = D // 2
     R = marks(C, G, D)[3]
     lane = W // T
-    S = T // 2
     flat = [x.reshape(rows, C) for x in (history, out_cotangent, skip_cotangent)]
     vmem = pl.BlockSpec(memory_space=pltpu.VMEM)
     hbm = pl.BlockSpec(memory_space=pl.ANY)
@@ -366,16 +341,15 @@
             V((G, C), BF16), V((G, C), BF16), V((rows, C), BF16), V((rows, C), BF16),
             V((rows, C), BF16), V((rows, C), BF16), V((rows, C), BF16),
             V((rows, C), BF16), V((rows, C), BF16), V((rows, C), BF16), V((rows, C), F32),
-            V((CHUNK, W), F32), V((CHUNK, G), F32), V((CHUNK, G), BF16), V((CHUNK, W), BF16),
+            V((CHUNK, W), F32), V((rows, G), F32), V((rows, G), BF16), V((rows, W), BF16),
             V((2 * C, W), F32), V((G, 2 * C), F32), V((1, W), F32),
-            V((H, 2, R, G), BF16), V((H, 2, R, G), BF16), V((H, 2, 2, R, G), F32),
-            V((H, R, G), BF16), V((H, R, G), BF16),
-            V((H - 1, R, G), BF16), V((H - 1, R, G), BF16),
-            V((S, R, lane), F32), V((S - 1, R, lane), BF16), V((S - 1, R, lane), BF16),
+            V((H, R, W), BF16), V((H, R, W), BF16), V((H, 2, R, W), F32),
+            V((H - 1, R, W), BF16), V((H - 1, R, W), BF16),
+            V((T, R, lane), F32), V((T - 1, R, lane), BF16), V((T - 1, R, lane), BF16),
             V((T, R, lane), BF16),
             dma((8,)), dma((3, K)), dma((K,)), dma((K,)), dma((K,)), dma((K,)),
-            dma((3,)), dma((3,)), dma((3,)), dma((3,)), dma((3, H - 1)), dma((3, H - 1)),
-            dma((3, S - 1)), dma((3, S - 1)), dma((3, T - 1)), dma((3, T - 1)),
+            dma((3,)), dma((3,)), dma((3, H - 1)), dma((3, H - 1)),
+            dma((3, T - 1)), dma((3, T - 1)), dma((3, T - 1)), dma((3, T - 1)),
         ],
         compiler_params=pltpu.CompilerParams(
             collective_id=0, has_side_effects=True, vmem_limit_bytes=60 * 1024 * 1024
@@ -395,7 +369,7 @@
             jax.ShapeDtypeStruct((G // D, C), F32),
             jax.ShapeDtypeStruct((G // D, C), F32),
         ],
-        in_specs=[hbm] * 3 + [vmem],
+        in_specs=[vmem] * 4,
         out_specs=[hbm] * 3 + [vmem] * 5,
         scratch_shapes=[dma((3,))],
         compiler_params=pltpu.CompilerParams(vmem_limit_bytes=60 * 1024 * 1024),

time: 175 us -> 67.4 us (0.39)
  Pallas kernels: 175 us -> 66.6 us
    pallas_call x1, Pallas kernels: 98.1 us -> 4.31 us  [shards(): pl.pallas_call(functools.partial(unpack_kernel, D), out_shape=[seq, seq,...]
    pallas_call x1, Pallas kernels: 76.4 us -> 62.3 us  [shards(): pl.pallas_call(functools.partial(layer_kernel, T, D), out_shape=[seq, seq...]
where the time goes in v4:
time: 67.4 us; the launch traced here: 67.3 us
  Pallas kernels  66.6 us (99%)
    pallas_call x1, Pallas kernels, shards(): pl.pallas_call(functools.partial(layer_kernel, T, D), out_shape=[seq, seq...  62.3 us
    pallas_call x1, Pallas kernels, shards(): pl.pallas_call(functools.partial(unpack_kernel, D), out_shape=[seq, seq,...  4.31 us

profile of v4, /device:TPU:0, one launch (start us, length us, event | category | flops | bytes accessed | tf_op | source)
XLA Modules:
  0.0 67.3 jit_solution(4788598925300929212)
XLA Ops:
  0.6 62.3 %gated_layer.1 = (bf16[2048,256]{1,0:T(8,128)(2,1)}, bf16[2048,256]{1,0:T(8,128)(2,1)}, bf16[2048,256]{1,0:T(8,128)(2,1)}, bf16[112,1024]{1,0:T(8,128)(2,1)}) custom-call(bf16[2048,256]{1,0:T(8,128)(2,1)} %bitcast.8, bf16[256,1024]{1,0:T(8,128)(2,1)} %now_h.1, bf16[256,1024]{1,0:T(8,128)(2,1)} %past_h.1, f32[1,1024]{1,0:T(1,128)} %bitcast.14, ...), custom_call_target="tpu_custom_call" | custom-call | flops 9663676416 | bytes 6291456 | tf_op jit(solution)/shard_map/gated_layer/pallas_call | solution.py:334
  63.0 4.3 %unpack_results.1 = (bf16[2048,256]{1,0:T(8,128)(2,1)}, bf16[2048,256]{1,0:T(8,128)(2,1)}, bf16[2048,256]{1,0:T(8,128)(2,1)}, f32[32,1024]{1,0:T(8,128)}, f32[32...) custom-call(bf16[2048,256]{1,0:T(8,128)(2,1)} %get-tuple-element.20.a, ...), custom_call_target="tpu_custom_call" | custom-call | bytes 6291456 | tf_op jit(solution)/shard_map/unpack_results/pallas_call | solution.py:362

commit v5 on v4

--- a/solution.py
+++ b/solution.py
@@ -9,7 +9,7 @@
 
 DILATION_STEPS = 2048
 CHUNK = 512
-BIAS_ROWS = 16
+BIAS_ROWS = 8
 F32 = jnp.float32
 BF16 = jnp.bfloat16
 MESH = pl.DeviceIdType.MESH
@@ -26,13 +26,14 @@
 def layer_kernel(
     T, D,
     hist_h, now_h, past_h, bias_h, res_h, skip_h, ocot_h, scot_h,
-    resid_h, skipped_h, grad_in_h, packed,
+    resid_h, skipped_h, grad_in_h, packed, bias_sum,
     hist, now_w, past_w, bias, res_w, skip_w, ocot, scot, resid, skipped, grad_in,
     delayed, bw_send, bw_recv, gi_part, zn, dgs, gated_s, dz_s,
     acc_np, acc_rs, acc_b, a_send, a_recv, b_own, b_send, b_recv,
-    tot, c_send, c_recv, d_buf,
+    tot, c_send, c_recv, d_buf, e_own, e_core, e_send, e_recv, e_all,
     in_s, out_s, f_ss, f_rs, w_ss, w_rs,
     a_ss, a_rs, b_ss, b_rs, c_ss, c_rs, d_ss, d_rs,
+    ea_ss, ea_rs, eb_ss, eb_rs, ec_ss, ec_rs,
 ):
     rows, C = hist.shape
     G = res_w.shape[0]
@@ -52,8 +53,8 @@
     W = 2 * G
     bw = W // D
     lane = W // T
-    r1, r2, r3, r4 = marks(C, G, D)
-    pieces = [(0, r1), (r1, r3), (r3, r4)]
+    r1, r2, r3 = marks(C, G, D)
+    pieces = [(0, r1), (r1, r2), (r2, r3)]
 
     loads = [
         pltpu.make_async_copy(x, y, in_s.at[i])
@@ -215,18 +216,39 @@
     add_now(last)
     for q in range(D):
         blk = b_own.at[q // 2, q % 2]
-        blk[r1:r2, :] = jnp.zeros((BIAS_ROWS, W), F32)
-        blk[r1:r1 + 1, 0:bw] = acc_b[:, q * bw:(q + 1) * bw]
-        blk[r2:r3, :] = acc_np[q * Rn:(q + 1) * Rn, :]
+        blk[r1:r2, :] = acc_np[q * Rn:(q + 1) * Rn, :]
+        e_own[q % 2, q // 2] = jnp.broadcast_to(acc_b[:, q * bw:(q + 1) * bw], (BIAS_ROWS, bw))
     core_send(1)
+    ea = remote(e_own.at[1 - par], e_core, ea_ss, ea_rs, {"dp": 2 * j0 + 1 - par})
+    ea.start()
     z_send(0)
     add_past(last)
     for q in range(D):
-        b_own[q // 2, q % 2, r3:r4, :] = acc_np[C + q * Rn:C + (q + 1) * Rn, :]
+        b_own[q // 2, q % 2, r2:r3, :] = acc_np[C + q * Rn:C + (q + 1) * Rn, :]
     core_send(2)
     z_send(1)
     z_send(2)
+    ea.wait_recv()
+    e_core[...] += e_own[par]
+    es = []
+    for o in range(1, H):
+        jt = lax.rem(j0 + o, H)
+        cp = remote(e_core.at[jt], e_recv.at[o - 1], eb_ss.at[o - 1], eb_rs.at[o - 1], {"dp": 2 * jt + par})
+        cp.start()
+        es.append(cp)
     lax.fori_loop(0, K, late, 0)
+    e_total = e_core[j0]
+    for cp in es:
+        cp.wait_recv()
+    for o in range(1, H):
+        e_total = e_total + e_recv[o - 1]
+    e_send[...] = e_total
+    e_all[me] = e_total
+    ec = []
+    for o in range(1, T):
+        cp = remote(e_send, e_all.at[me], ec_ss.at[o - 1], ec_rs.at[o - 1], {"tm": lax.rem(me + o, T)})
+        cp.start()
+        ec.append(cp)
 
     for p, (lo, hi) in enumerate(pieces):
         total = pair_sum(j0, lo, hi)
@@ -281,9 +303,16 @@
             t = lax.rem(me + T - o, T)
             remote(d_buf.at[t, lo:hi, :], d_buf.at[t, lo:hi, :], d_ss.at[p, o - 1], d_rs.at[p, o - 1],
                    {"tm": lax.rem(me + o, T)}).wait_recv()
+    for o in range(1, T):
+        remote(e_send, e_all.at[lax.rem(me + T - o, T)], ec_ss.at[o - 1], ec_rs.at[o - 1],
+               {"tm": lax.rem(me + o, T)}).wait_recv()
+    e_full = e_all[0]
+    for t in range(1, T):
+        e_full = e_full + e_all[t]
+    bias_sum[...] = e_full
     for t in range(T):
         packed[:, t * lane:(t + 1) * lane] = d_buf[t]
-    for cp in cores + zs + cs + ds:
+    for cp in [ea] + es + ec + cores + zs + cs + ds:
         cp.wait_send()
     for c in range(K):
         store(2, c).wait()
@@ -291,27 +320,33 @@
 
 def marks(C, G, D):
     r1 = G // D // 2
-    r2 = r1 + BIAS_ROWS
-    r3 = r2 + C // D
-    return r1, r2, r3, r3 + C // D
-
-
-def unpack_kernel(D, a, b, c, packed, oa, ob, oc, g_now, g_past, g_bias, g_res, g_skip, sems):
-    copies = [pltpu.make_async_copy(x, y, sems.at[i]) for i, (x, y) in enumerate(((a, oa), (b, ob), (c, oc)))]
-    for cp in copies:
-        cp.start()
-    C = a.shape[1]
+    return r1, r1 + C // D, r1 + 2 * (C // D)
+
+
+def unpack_kernel(D, a, b, c, packed, bias_sum, oa, ob, oc, g_now, g_past, g_bias, g_res, g_skip, held, l_s, s_s):
+    rows, C = a.shape
+    K = rows // CHUNK
+    moves = []
+    for i, (x, y) in enumerate(((a, oa), (b, ob), (c, oc))):
+        for k in range(K):
+            at = pl.ds(k * CHUNK, CHUNK)
+            load = pltpu.make_async_copy(x.at[at], held.at[i, at], l_s.at[i, k])
+            load.start()
+            moves.append((load, pltpu.make_async_copy(held.at[i, at], y.at[at], s_s.at[i, k])))
     G = packed.shape[1] // 2
-    r1, r2, r3, r4 = marks(C, G, D)
-    g_bias[...] = packed[r1:r2, 0:2 * G // D].astype(F32)[0:1]
+    r1, r2, r3 = marks(C, G, D)
+    g_bias[...] = bias_sum[0:1, :]
     for half in range(2):
         at = 2 * C * half
         g_res[half * r1:(half + 1) * r1, :] = packed[0:r1, at:at + C].astype(F32)
         g_skip[half * r1:(half + 1) * r1, :] = packed[0:r1, at + C:at + 2 * C].astype(F32)
-    g_now[...] = packed[r2:r3, :].astype(F32)
-    g_past[...] = packed[r3:r4, :].astype(F32)
-    for cp in copies:
-        cp.wait()
+    g_now[...] = packed[r1:r2, :].astype(F32)
+    g_past[...] = packed[r2:r3, :].astype(F32)
+    for load, put in moves:
+        load.wait()
+        put.start()
+    for load, put in moves:
+        put.wait()
 
 
 def shards(T, D, history, now_weight, past_weight, gate_bias, residual_weight, skip_weight,
@@ -323,7 +358,8 @@
     W = 2 * G
     K = rows // CHUNK
     H = D // 2
-    R = marks(C, G, D)[3]
+    R = marks(C, G, D)[2]
+    bw = W // D
     lane = W // T
     flat = [x.reshape(rows, C) for x in (history, out_cotangent, skip_cotangent)]
     vmem = pl.BlockSpec(memory_space=pltpu.VMEM)
@@ -333,9 +369,10 @@
     seq = jax.ShapeDtypeStruct((rows, C), BF16)
     parts = pl.pallas_call(
         functools.partial(layer_kernel, T, D),
-        out_shape=[seq, seq, seq, jax.ShapeDtypeStruct((R, W), BF16)],
+        out_shape=[seq, seq, seq, jax.ShapeDtypeStruct((R, W), BF16),
+                   jax.ShapeDtypeStruct((BIAS_ROWS, bw), F32)],
         in_specs=[hbm] * 8,
-        out_specs=[hbm] * 3 + [vmem],
+        out_specs=[hbm] * 3 + [vmem] * 2,
         scratch_shapes=[
             V((rows, C), BF16), V((C, W), BF16), V((C, W), BF16), V((1, W), F32),
             V((G, C), BF16), V((G, C), BF16), V((rows, C), BF16), V((rows, C), BF16),
@@ -347,9 +384,12 @@
             V((H - 1, R, W), BF16), V((H - 1, R, W), BF16),
             V((T, R, lane), F32), V((T - 1, R, lane), BF16), V((T - 1, R, lane), BF16),
             V((T, R, lane), BF16),
+            V((2, H, BIAS_ROWS, bw), F32), V((H, BIAS_ROWS, bw), F32), V((BIAS_ROWS, bw), F32),
+            V((H - 1, BIAS_ROWS, bw), F32), V((T, BIAS_ROWS, bw), F32),
             dma((8,)), dma((3, K)), dma((K,)), dma((K,)), dma((K,)), dma((K,)),
             dma((3,)), dma((3,)), dma((3, H - 1)), dma((3, H - 1)),
             dma((3, T - 1)), dma((3, T - 1)), dma((3, T - 1)), dma((3, T - 1)),
+            dma, dma, dma((H - 1,)), dma((H - 1,)), dma((T - 1,)), dma((T - 1,)),
         ],
         compiler_params=pltpu.CompilerParams(
             collective_id=0, has_side_effects=True, vmem_limit_bytes=60 * 1024 * 1024
@@ -369,9 +409,9 @@
             jax.ShapeDtypeStruct((G // D, C), F32),
             jax.ShapeDtypeStruct((G // D, C), F32),
         ],
-        in_specs=[vmem] * 4,
+        in_specs=[hbm] * 3 + [vmem] * 2,
         out_specs=[hbm] * 3 + [vmem] * 5,
-        scratch_shapes=[dma((3,))],
+        scratch_shapes=[V((3, rows, C), BF16), dma((3, K)), dma((3, K))],
         compiler_params=pltpu.CompilerParams(vmem_limit_bytes=60 * 1024 * 1024),
         cost_estimate=pl.CostEstimate(flops=0, bytes_accessed=rows * C * 12, transcendentals=0),
         name="unpack_results",

time: 67.4 us -> 67.8 us (level)
  no operation moved by 1% of the time
where the time goes in v5:
time: 67.8 us; the launch traced here: 67.6 us
  Pallas kernels  67 us (99%)
    pallas_call x1, Pallas kernels, shards(): pl.pallas_call(functools.partial(layer_kernel, T, D), out_shape=[seq, seq...  62.5 us
    pallas_call x1, Pallas kernels, shards(): pl.pallas_call(functools.partial(unpack_kernel, D), out_shape=[seq, seq,...  4.48 us

profile of v5, /device:TPU:0, one launch (start us, length us, event | category | flops | bytes accessed | tf_op | source)
XLA Modules:
  0.0 67.6 jit_solution(5390270764867680148)
XLA Ops:
  0.6 62.5 %gated_layer.1 = (bf16[2048,256]{1,0:T(8,128)(2,1)}, bf16[2048,256]{1,0:T(8,128)(2,1)}, bf16[2048,256]{1,0:T(8,128)(2,1)}, bf16[96,1024]{1,0:T(8,128)(2,1)}, f32[8,128]{1,0:T(8,128)}) custom-call(bf16[2048,256]{1,0:T(8,128)(2,1)} %bitcast.8, bf16[256,1024]{1,0:T(8,128)(2,1)} %now_h.1, bf16[256,1024]{1,0:T(8,128)(2,1)} %past_h.1, f32[1,1024]{1,0:T(1,128)} %bitcast.14, ...), custom_call_target="tpu_custom_call" | custom-call | flops 9663676416 | bytes 6291456 | tf_op jit(solution)/shard_map/gated_layer/pallas_call | solution.py:370
  63.2 4.5 %unpack_results.1 = (bf16[2048,256]{1,0:T(8,128)(2,1)}, bf16[2048,256]{1,0:T(8,128)(2,1)}, bf16[2048,256]{1,0:T(8,128)(2,1)}, f32[32,1024]{1,0:T(8,128)}, f32[32...) custom-call(bf16[2048,256]{1,0:T(8,128)(2,1)} %get-tuple-element.21.a, ...), custom_call_target="tpu_custom_call" | custom-call | bytes 6291456 | tf_op jit(solution)/shard_map/unpack_results/pallas_call | solution.py:402

commit v6 on v4

--- a/solution.py
+++ b/solution.py
@@ -8,7 +8,7 @@
 from jax.sharding import PartitionSpec as P
 
 DILATION_STEPS = 2048
-CHUNK = 512
+CHUNK = 256
 BIAS_ROWS = 16
 F32 = jnp.float32
 BF16 = jnp.bfloat16

time: 67.4 us -> 66.6 us (0.988)
  Pallas kernels: 66.6 us -> 65.8 us
    pallas_call x1, Pallas kernels: 62.3 us -> 61.5 us  [shards(): pl.pallas_call(functools.partial(layer_kernel, T, D), out_shape=[seq, seq...]
where the time goes in v6:
time: 66.6 us; the launch traced here: 66.5 us
  Pallas kernels  65.8 us (99%)
    pallas_call x1, Pallas kernels, shards(): pl.pallas_call(functools.partial(layer_kernel, T, D), out_shape=[seq, seq...  61.5 us
    pallas_call x1, Pallas kernels, shards(): pl.pallas_call(functools.partial(unpack_kernel, D), out_shape=[seq, seq,...  4.31 us

profile of v6, /device:TPU:0, one launch (start us, length us, event | category | flops | bytes accessed | tf_op | source)
XLA Modules:
  0.0 66.5 jit_solution(13586149716183373342)
XLA Ops:
  0.6 61.5 %gated_layer.1 = (bf16[2048,256]{1,0:T(8,128)(2,1)}, bf16[2048,256]{1,0:T(8,128)(2,1)}, bf16[2048,256]{1,0:T(8,128)(2,1)}, bf16[112,1024]{1,0:T(8,128)(2,1)}) custom-call(bf16[2048,256]{1,0:T(8,128)(2,1)} %bitcast.8, bf16[256,1024]{1,0:T(8,128)(2,1)} %now_h.1, bf16[256,1024]{1,0:T(8,128)(2,1)} %past_h.1, f32[1,1024]{1,0:T(1,128)} %bitcast.14, ...), custom_call_target="tpu_custom_call" | custom-call | flops 9663676416 | bytes 6291456 | tf_op jit(solution)/shard_map/gated_layer/pallas_call | solution.py:334
  62.1 4.3 %unpack_results.1 = (bf16[2048,256]{1,0:T(8,128)(2,1)}, bf16[2048,256]{1,0:T(8,128)(2,1)}, bf16[2048,256]{1,0:T(8,128)(2,1)}, f32[32,1024]{1,0:T(8,128)}, f32[32...) custom-call(bf16[2048,256]{1,0:T(8,128)(2,1)} %get-tuple-element.20.a, ...), custom_call_target="tpu_custom_call" | custom-call | bytes 6291456 | tf_op jit(solution)/shard_map/unpack_results/pallas_call | solution.py:362
